TPU v7x, 768 devices: a whole 4x8x12 slice. The times are simulated.
768 devices in a mesh: dp: 24 (over x_hi, z), expert: 32 (over y, x_lo, core).
Axes of the slice: x: 4 (x_hi: 2, x_lo: 2; x = x_hi * 2 + x_lo), y: 8, z: 12, core: 2. Of those that a mesh axis runs over, the one named last changes fastest.
Arguments:
- token_rows: bfloat16 [49152, 4096], P(('dp', 'expert')), may hold values from -6 to 6
- row_scales: bfloat16 [49152], P(('dp', 'expert')), may hold values from 0.099609375 to 2
- expert_ids: int32 [49152, 8], P(('dp', 'expert')), may hold values from 0 to 127, all different within a row; in each aligned block of 64 rows (0 to 63, 64 to 127, ...) at most 5 rows name the same one
- gate_values: bfloat16 [49152, 8], P(('dp', 'expert')), may hold values from 0.049804688 to 0.59765625
- upstream: bfloat16 [49152, 8, 768], P(('dp', 'expert')), may hold values from -6 to 6
- weight: bfloat16 [32, 4096, 768], P('expert'), may hold values from -0.09375 to 0.09375
Outputs:
- token_grads: bfloat16 [49152, 4096], P(('dp', 'expert'))
- gate_grads: bfloat16 [49152, 8], P(('dp', 'expert'))
- weight_grads: float32 [32, 4096, 768], P('expert', None, 'dp')
Inputs may be any that keep to these rules, and one draw needn't show every extreme that they name: `expert_ids`: each row names 8 different experts; among the 64 rows of one device no expert is named more than 5 times.
All inputs are finite; a program needn't handle non-finite values.
Results may differ from a plain program's by a relative error of at most 0.02.
Values may be sent and summed in bfloat16 or wider, within the bound.
No kernel may reach another device: no remote copies, remote signals or barrier semaphores. Data moves between devices by JAX's collectives and lax.ppermute only.
A program may use at most 64 MiB of HBM per device.

v0:
```python
import jax
import jax.numpy as jnp
from jax import lax
from jax.sharding import PartitionSpec as P

CAP = 5


def local(token_rows, row_scales, expert_ids, gate_values, upstream, weight):
    tok_count = token_rows.shape[0]
    pick_count = expert_ids.shape[1]
    width = token_rows.shape[1]
    hidden_width = upstream.shape[2]
    experts_here = lax.axis_size("expert")
    slot_count = experts_here * CAP
    choice_count = tok_count * pick_count
    dequant = (row_scales.astype(jnp.float32)[:, None] * token_rows.astype(jnp.float32)).astype(
        jnp.bfloat16
    )
    ids_flat = expert_ids.reshape(choice_count)
    onehot = (ids_flat[:, None] == jnp.arange(experts_here, dtype=jnp.int32)[None, :]).astype(
        jnp.int32
    )
    before = jnp.cumsum(onehot, axis=0) - onehot
    slot_index = jnp.sum(before * onehot, axis=1)
    is_live = jnp.sum(onehot, axis=1)
    position = jnp.where(is_live > 0, ids_flat * CAP + slot_index, -1)
    placing = (position[:, None] == jnp.arange(slot_count, dtype=jnp.int32)[None, :]).astype(
        jnp.int32
    )
    up_flat = upstream.reshape(choice_count, hidden_width)
    gate_flat = gate_values.reshape(choice_count)
    place_bf = placing.astype(jnp.bfloat16)
    token_place = jnp.sum(placing.reshape(tok_count, pick_count, slot_count), axis=1).astype(
        jnp.bfloat16
    )
    send_rows = jnp.dot(token_place.T, dequant, preferred_element_type=jnp.float32).astype(
        jnp.bfloat16
    )
    send_up = jnp.dot(place_bf.T, up_flat, preferred_element_type=jnp.float32).astype(jnp.bfloat16)
    send_gate = jnp.dot(place_bf.T, gate_flat, preferred_element_type=jnp.float32).astype(
        jnp.bfloat16
    )
    recv_rows, recv_up, recv_gate = (
        lax.all_to_all(
            send_rows.reshape(experts_here, CAP, width),
            "expert",
            split_axis=0,
            concat_axis=0,
            tiled=True,
        ),
        lax.all_to_all(
            send_up.reshape(experts_here, CAP, hidden_width),
            "expert",
            split_axis=0,
            concat_axis=0,
            tiled=True,
        ),
        lax.all_to_all(
            send_gate.reshape(experts_here, CAP), "expert", split_axis=0, concat_axis=0, tiled=True
        ),
    )
    rows_in = recv_rows.reshape(slot_count, width)
    up_in = recv_up.reshape(slot_count, hidden_width)
    gate_in = recv_gate.reshape(slot_count)
    matrix = weight[0]
    out_grad = (gate_in.astype(jnp.float32)[:, None] * up_in.astype(jnp.float32)).astype(
        jnp.bfloat16
    )
    recomputed = jnp.dot(rows_in, matrix, preferred_element_type=jnp.float32)
    gate_terms = jnp.sum(up_in.astype(jnp.float32) * recomputed, axis=1).astype(jnp.bfloat16)
    row_grads = lax.dot_general(
        out_grad, matrix, (((1,), (1,)), ((), ())), preferred_element_type=jnp.float32
    ).astype(jnp.bfloat16)
    back_rows, back_gate = (
        lax.all_to_all(
            row_grads.reshape(experts_here, CAP, width),
            "expert",
            split_axis=0,
            concat_axis=0,
            tiled=True,
        ),
        lax.all_to_all(
            gate_terms.reshape(experts_here, CAP), "expert", split_axis=0, concat_axis=0, tiled=True
        ),
    )
    partial_grad = lax.dot_general(
        rows_in, out_grad, (((0,), (0,)), ((), ())), preferred_element_type=jnp.float32
    )
    weight_grads = lax.psum_scatter(
        partial_grad.astype(jnp.bfloat16), "dp", scatter_dimension=1, tiled=True
    ).astype(jnp.float32)
    back_rows = back_rows.reshape(slot_count, width)
    back_gate = back_gate.reshape(slot_count)
    token_place = jnp.sum(placing.reshape(tok_count, pick_count, slot_count), axis=1).astype(
        jnp.bfloat16
    )
    token_grads = jnp.dot(token_place, back_rows, preferred_element_type=jnp.float32).astype(
        jnp.bfloat16
    )
    gate_grads = jnp.dot(
        placing.astype(jnp.float32), back_gate.astype(jnp.float32), precision=lax.Precision.HIGHEST
    )
    gate_grads = gate_grads.reshape(tok_count, pick_count).astype(jnp.bfloat16)
    return (token_grads, gate_grads, weight_grads[None])


def solution(mesh):
    in_specs = (
        P(("dp", "expert"), None),
        P(("dp", "expert")),
        P(("dp", "expert"), None),
        P(("dp", "expert"), None),
        P(("dp", "expert"), None, None),
        P("expert", None, None),
    )
    out_specs = (P(("dp", "expert"), None), P(("dp", "expert"), None), P("expert", None, "dp"))
    return jax.shard_map(local, mesh=mesh, in_specs=in_specs, out_specs=out_specs, check_vma=False)
```

profile of v0, /device:TPU:1, one launch (start us, length us, event | category | flops | bytes accessed | tf_op | source)
XLA Modules:
  0.0 509.5 jit_solution(8356913526006382721)
XLA Ops:
  7.2 0.0 copy-start
  7.2 0.0 copy-start.4
  7.2 0.0 copy-start.5
  7.2 0.0 copy-start.3
  7.2 0.9 copy.43
  8.1 0.1 eq.76
  8.2 0.1 eq.72
  8.3 1.2 reduce-window.6
  9.4 0.2 slice_reduce_fusion
  9.7 0.8 copy.49
  10.5 0.1 reshape.161
  10.6 0.1 fusion.25
  10.7 0.1 fusion.22
  10.9 0.7 all_to_all.25
  11.6 14.0 %all-to-all-start = ((bf16[32,1,5]{2,1,0:T(2,128)(2,1)}), bf16[32,1,5]{2,1,0:T(2,128)(2,1)S(1)}, u32[]{:S(2)}, u32[]{:S(2)}) async-start(bf16[32,1,5]{2,1,0:T(2,128)(2,1)} %all_to_all.25), calls=%async_computation | async-start | bytes 32768 | tf_op jit(solution)/shard_map/all_to_all | solution.py:59
  25.6 0.0 copy-done
  25.6 0.4 convolution_convert_fusion.2
  26.1 0.1 reduce_sum.44
  26.2 0.1 gt.16
  26.3 0.1 copy.47
  26.3 0.1 copy.46
  26.4 0.9 reshape.152
  27.3 6.3 %all-to-all-done = bf16[32,1,5]{2,1,0:T(2,128)(2,1)S(1)} async-done(((bf16[32,1,5]{2,1,0:T(2,128)(2,1)}), bf16[32,1,5]{2,1,0:T(2,128)(2,1)S(1)}, u32[]{:S(2)}, u32[]{:S(2)}) %all-to-all-start) | async-done | bytes 352 | tf_op jit(solution)/shard_map/all_to_all | solution.py:59
  33.5 4.1 all-to-all-start.1
  37.6 0.0 copy-done.4
  37.7 0.1 copy.48
  37.8 0.0 copy-done.5
  37.8 0.2 convert_reduce_fusion
  38.0 0.0 copy-done.3
  38.0 0.6 convolution_convert_fusion
  38.6 1.6 reshape.155
  40.2 11.3 %all-to-all-done.1 = bf16[32,5,768]{2,1,0:T(8,128)(2,1)S(1)} async-done(((bf16[32,5,768]{2,1,0:T(8,128)(2,1)}), bf16[32,5,768]{2,1,0:T(8,128)(2,1)S(1)}, u32[]{:S(2)}, u32[]{:S(2)}) %all-to-all-start.1) | async-done | bytes 245792 | tf_op jit(solution)/shard_map/all_to_all | solution.py:52
  51.6 5.3 %all-to-all-start.3 = ((bf16[32,5,4096]{2,1,0:T(8,128)(2,1)}), bf16[32,5,4096]{2,1,0:T(8,128)(2,1)S(1)}, u32[]{:S(2)}, u32[]{:S(2)}) async-start(bf16[32,5,4096]{2,1,0:T(8,128)(2,1)} %reshape.155), calls=%async_computation.3 | async-start | bytes 4194304 | tf_op jit(solution)/shard_map/all_to_all | solution.py:45
  56.9 0.0 reduce-scatter.2.cloned.1.call-start
  56.9 0.9 multiply_convert_fusion.1
  57.8 49.1 %all-to-all-done.3 = bf16[32,5,4096]{2,1,0:T(8,128)(2,1)S(1)} async-done(((bf16[32,5,4096]{2,1,0:T(8,128)(2,1)}), bf16[32,5,4096]{2,1,0:T(8,128)(2,1)S(1)}, u32[]{:S(2)}, u32[]{:S(2)}) %all-to-all-start.3) | async-done | bytes 1310752 | tf_op jit(solution)/shard_map/all_to_all | solution.py:45
  106.9 5.6 %bitcast_convert_fusion = bf16[4096,768]{0,1:T(8,128)(2,1)} fusion(bf16[32,5,4096]{2,1,0:T(8,128)(2,1)S(1)} %all-to-all-done.3, bf16[32,5,768]{2,1,0:T(8,128)(2,1)} %multiply_convert_fusion.1), kind=kOutput, calls=%fused_computation | convolution fusion | flops 1009778688 | bytes 7847936 | tf_op jit(solution)/shard_map/dot_general | solution.py:87
  112.5 0.0 reduce-scatter.2.cloned.1.call-update
  112.6 1.8 convert_element_type.149
  114.4 0.9 reshape.159
  115.2 0.0 copy-start.1
  115.2 1.4 reshape.156
  116.7 0.0 copy-done.1
  116.7 0.0 copy-start.2
  116.7 4.5 fusion.11
  121.2 0.7 convert_element_type.167
  121.9 5.5 %all-to-all-start.4 = ((bf16[32,1,5]{2,1,0:T(2,128)(2,1)}), bf16[32,1,5]{2,1,0:T(2,128)(2,1)S(1)}, u32[]{:S(2)}, u32[]{:S(2)}) async-start(bf16[32,1,5]{2,1,0:T(2,128)(2,1)} %convert_element_type.167), calls=%async_computation.4 | async-start | bytes 32768 | tf_op jit(solution)/shard_map/all_to_all | solution.py:83
  127.4 0.0 copy-done.2
  127.4 5.2 %fusion.4 = bf16[160,4096]{1,0:T(8,128)(2,1)S(1)} fusion(bf16[160,768]{1,0:T(8,128)(2,1)S(1)} %copy-done.2, bf16[1,4096,768]{2,1,0:T(8,128)(2,1)} %param.11), kind=kOutput, calls=%fused_computation.5 | convolution fusion | flops 1007288320 | bytes 7847936 | tf_op jit(solution)/shard_map/dot_general | solution.py:72
  132.6 1.6 reshape.153
  134.2 1.1 all-to-all-done.4
  135.3 7.3 %all-to-all-start.2 = ((bf16[32,5,4096]{2,1,0:T(8,128)(2,1)}), bf16[32,5,4096]{2,1,0:T(8,128)(2,1)S(1)}, u32[]{:S(2)}, u32[]{:S(2)}) async-start(bf16[32,5,4096]{2,1,0:T(8,128)(2,1)} %reshape.153), calls=%async_computation.2 | async-start | bytes 4194304 | tf_op jit(solution)/shard_map/all_to_all | solution.py:76
  142.6 0.7 fusion.15
  143.3 0.1 reduce.1
  143.4 0.1 reshape.163
  143.5 1.8 fusion.16
  145.3 0.7 copy.55
  146.0 46.7 %all-to-all-done.2 = bf16[32,5,4096]{2,1,0:T(8,128)(2,1)S(1)} async-done(((bf16[32,5,4096]{2,1,0:T(8,128)(2,1)}), bf16[32,5,4096]{2,1,0:T(8,128)(2,1)S(1)}, u32[]{:S(2)}, u32[]{:S(2)}) %all-to-all-start.2) | async-done | bytes 1310752 | tf_op jit(solution)/shard_map/all_to_all | solution.py:76
  192.6 1.4 reshape.154
  194.1 2.5 convolution_convert_fusion.1
  196.5 304.4 %reduce-scatter.2.cloned.1.call-done = bf16[4096,32]{0,1:T(8,128)(2,1)} async-done(((bf16[4096,768]{0,1:T(8,128)(2,1)}), bf16[4096,32]{0,1:T(8,128)(2,1)}) %reduce-scatter.2.cloned.1.call-update) | async-done | bytes 262160 | tf_op jit(solution)/shard_map/reduce_scatter | solution.py:90
  500.9 1.8 bitcast_convert_fusion.1
  (8 shorter events, 0.1 us)
Async XLA Ops:
  7.2 18.5 %copy-start = (bf16[64,8,768]{2,1,0:T(8,128)(2,1)S(1)}, bf16[64,8,768]{2,1,0:T(8,128)(2,1)}, u32[]{:S(2)}) copy-start(bf16[64,8,768]{2,1,0:T(8,128)(2,1)} %param.10) | copy-start | bytes 2359300
  7.2 30.5 %copy-start.4 = (s32[64,8]{0,1:T(8,128)S(1)}, s32[64,8]{0,1:T(8,128)}, u32[]{:S(2)}) copy-start(s32[64,8]{0,1:T(8,128)} %param.8) | copy-start | bytes 6148
  7.2 30.6 %copy-start.5 = (bf16[64]{0:T(256)(128)(2,1)S(1)}, bf16[64]{0:T(256)(128)(2,1)}, u32[]{:S(2)}) copy-start(bf16[64]{0:T(256)(128)(2,1)} %param.7) | copy-start | bytes 388
  7.2 30.8 %copy-start.3 = (bf16[64,4096]{1,0:T(8,128)(2,1)S(1)}, bf16[64,4096]{1,0:T(8,128)(2,1)}, u32[]{:S(2)}) copy-start(bf16[64,4096]{1,0:T(8,128)(2,1)} %param.6) | copy-start | bytes 1572868
  11.6 21.9 %all-to-all-start = ((bf16[32,1,5]{2,1,0:T(2,128)(2,1)}), bf16[32,1,5]{2,1,0:T(2,128)(2,1)S(1)}, u32[]{:S(2)}, u32[]{:S(2)}) async-start(bf16[32,1,5]{2,1,0:T(2,128)(2,1)} %all_to_all.25), calls=%async_computation | async-start | bytes 32768 | tf_op jit(solution)/shard_map/all_to_all | solution.py:59
  33.5 18.0 %all-to-all-start.1 = ((bf16[32,5,768]{2,1,0:T(8,128)(2,1)}), bf16[32,5,768]{2,1,0:T(8,128)(2,1)S(1)}, u32[]{:S(2)}, u32[]{:S(2)}) async-start(bf16[32,5,768]{2,1,0:T(8,128)(2,1)} %reshape.152), calls=%async_computation.1 | async-start | bytes 786432 | tf_op jit(solution)/shard_map/all_to_all | solution.py:52
  51.6 55.4 %all-to-all-start.3 = ((bf16[32,5,4096]{2,1,0:T(8,128)(2,1)}), bf16[32,5,4096]{2,1,0:T(8,128)(2,1)S(1)}, u32[]{:S(2)}, u32[]{:S(2)}) async-start(bf16[32,5,4096]{2,1,0:T(8,128)(2,1)} %reshape.155), calls=%async_computation.3 | async-start | bytes 4194304 | tf_op jit(solution)/shard_map/all_to_all | solution.py:45
  56.9 444.0 %reduce-scatter.2.cloned.1.call-start = ((), (), s32[]{:S(2)}) async-start(), calls=%async_computation.6 | async-start | bytes 6553600 | tf_op jit(solution)/shard_map/reduce_scatter | solution.py:90
  115.2 1.4 copy-start.1
  116.7 10.7 %copy-start.2 = (bf16[160,768]{1,0:T(8,128)(2,1)S(1)}, bf16[160,768]{1,0:T(8,128)(2,1)}, u32[]{:S(2)}) copy-start(bf16[160,768]{1,0:T(8,128)(2,1)} %convert_element_type.149) | copy-start | bytes 737284
  121.9 13.4 %all-to-all-start.4 = ((bf16[32,1,5]{2,1,0:T(2,128)(2,1)}), bf16[32,1,5]{2,1,0:T(2,128)(2,1)S(1)}, u32[]{:S(2)}, u32[]{:S(2)}) async-start(bf16[32,1,5]{2,1,0:T(2,128)(2,1)} %convert_element_type.167), calls=%async_computation.4 | async-start | bytes 32768 | tf_op jit(solution)/shard_map/all_to_all | solution.py:83
  135.3 57.4 %all-to-all-start.2 = ((bf16[32,5,4096]{2,1,0:T(8,128)(2,1)}), bf16[32,5,4096]{2,1,0:T(8,128)(2,1)S(1)}, u32[]{:S(2)}, u32[]{:S(2)}) async-start(bf16[32,5,4096]{2,1,0:T(8,128)(2,1)} %reshape.153), calls=%async_computation.2 | async-start | bytes 4194304 | tf_op jit(solution)/shard_map/all_to_all | solution.py:76
Sparse Core Ops, SparseCore 0:
  112.7 388.1 reduce-scatter.1
where the time goes:
time: 516 us; the launch traced here: 509 us
  waiting for transfers between devices  419 us (81%)
  starting transfers between devices  36.2 us (7%)
  matrix products  20.7 us (4%)
  local copies, waits for them, and re-layouts  14.5 us (3%)
  between operations  14.2 us (3%)
    reduce_scatter x1, waiting for transfers between devices, local(): lax.psum_scatter(partial_grad.astype(jnp.bfloat16), 'dp', scatter_dimensi...  304 us
    all_to_all x1, waiting for transfers between devices, local(): lax.all_to_all(send_rows.reshape(experts_here, CAP, width), 'expert', spl...  49.1 us
    all_to_all x1, waiting for transfers between devices, local(): lax.all_to_all(row_grads.reshape(experts_here, CAP, width), 'expert', spl...  46.7 us
    all_to_all x1, starting transfers between devices, local(): lax.all_to_all(send_gate.reshape(experts_here, CAP), 'expert', split_axis...  14 us
    all_to_all x1, waiting for transfers between devices, local(): lax.all_to_all(send_up.reshape(experts_here, CAP, hidden_width), 'expert'...  11.3 us
  transfers between devices with their start and end apart: 6, of which 6 were waited for; matrix products, arithmetic and copies ran while one was open for 6% of the time, Pallas kernels for 0%

commit v1 on v0

v1 whole, which is shorter than its diff:
```python
import jax
import jax.numpy as jnp
from jax import lax
from jax.sharding import Mesh, PartitionSpec as P

CAP = 5
LANE = 128
EXPERT_AXES = ("y", "xl", "c")
ALL_AXES = ("xh", "z") + EXPERT_AXES


def dot_t(a, b):
    return lax.dot_general(a, b, (((0,), (0,)), ((), ())), preferred_element_type=jnp.float32)


def local(token_rows, row_scales, expert_ids, gate_values, upstream, weight):
    toks, picks = expert_ids.shape
    width = token_rows.shape[1]
    hidden = upstream.shape[2]
    experts = lax.axis_size(EXPERT_AXES)
    slots = experts * CAP
    choices = toks * picks
    half = hidden // 2
    x_lines = CAP * width // LANE
    dz_lines = CAP * hidden // LANE

    x = (row_scales.astype(jnp.float32)[:, None] * token_rows.astype(jnp.float32)).astype(
        jnp.bfloat16
    )
    dz = (gate_values.astype(jnp.float32)[..., None] * upstream.astype(jnp.float32)).astype(
        jnp.bfloat16
    )
    ids = expert_ids.reshape(choices)
    onehot = (ids[:, None] == jnp.arange(experts, dtype=jnp.int32)[None, :]).astype(jnp.int32)
    before = jnp.cumsum(onehot, axis=0) - onehot
    slot = jnp.sum(before * onehot, axis=1)
    position = jnp.where(ids < experts, ids * CAP + slot, -1)
    placing = position[:, None] == jnp.arange(slots, dtype=jnp.int32)[None, :]
    place = placing.astype(jnp.bfloat16)
    token_place = jnp.sum(
        placing.astype(jnp.int32).reshape(toks, picks, slots), axis=1
    ).astype(jnp.bfloat16)

    send_x = dot_t(token_place, x).astype(jnp.bfloat16)
    send_dz = dot_t(place, dz.reshape(choices, hidden)).astype(jnp.bfloat16)
    pad = (-(x_lines + dz_lines)) % 16
    message = jnp.concatenate(
        [
            send_x.reshape(experts, x_lines, LANE),
            send_dz.reshape(experts, dz_lines, LANE),
            jnp.zeros((experts, pad, LANE), jnp.bfloat16),
        ],
        axis=1,
    )
    mine = lax.all_to_all(message, EXPERT_AXES, 0, 0, tiled=True)
    other = lax.ppermute(mine, "xh", [(0, 1), (1, 0)])

    def unpack(raw):
        rows = raw[:, :x_lines].reshape(slots, width)
        grads = raw[:, x_lines : x_lines + dz_lines].reshape(slots, hidden)
        return rows, grads

    x_in, dz_in = unpack(mine)
    matrix = weight[0]
    row_grads = lax.dot_general(
        dz_in, matrix, (((1,), (1,)), ((), ())), preferred_element_type=jnp.float32
    ).astype(jnp.bfloat16)
    z = jnp.dot(x_in, matrix, preferred_element_type=jnp.float32)
    terms = jnp.sum(dz_in.astype(jnp.float32) * z, axis=1).astype(jnp.bfloat16)
    reply = jnp.concatenate(
        [
            row_grads.reshape(experts, x_lines, LANE),
            jnp.pad(terms.reshape(experts, 1, CAP), ((0, 0), (0, 15), (0, LANE - CAP))),
        ],
        axis=1,
    )
    back = lax.all_to_all(reply, EXPERT_AXES, 0, 0, tiled=True)

    x_other, dz_other = unpack(other)
    at = lax.axis_index("xh") * half
    x_both = jnp.concatenate([x_in, x_other], axis=0)
    dz_both = jnp.concatenate(
        [
            lax.dynamic_slice_in_dim(dz_in, at, half, 1),
            lax.dynamic_slice_in_dim(dz_other, at, half, 1),
        ],
        axis=0,
    )
    partial = dot_t(dz_both, x_both).astype(jnp.bfloat16)
    weight_grads = lax.psum_scatter(partial, "z", scatter_dimension=0, tiled=True)

    back_rows = back[:, :x_lines].reshape(slots, width)
    back_terms = back[:, x_lines, :CAP].reshape(slots).astype(jnp.float32)
    token_grads = jnp.dot(token_place, back_rows, preferred_element_type=jnp.float32).astype(
        jnp.bfloat16
    )
    picked = jnp.sum(jnp.where(placing, back_terms[None, :], 0.0), axis=1)
    gate_grads = (picked.reshape(toks, picks) / gate_values.astype(jnp.float32)).astype(
        jnp.bfloat16
    )
    return token_grads, gate_grads, weight_grads.astype(jnp.float32).T[None]


def solution(mesh):
    n_dp, n_expert = mesh.shape["dp"], mesh.shape["expert"]
    fine = Mesh(mesh.devices.reshape(2, n_dp // 2, n_expert // 4, 2, 2), ALL_AXES)
    rows = P(ALL_AXES)
    in_specs = (rows, rows, rows, rows, rows, P(EXPERT_AXES))
    out_specs = (rows, rows, P(EXPERT_AXES, None, ("xh", "z")))
    return jax.shard_map(
        local, mesh=fine, in_specs=in_specs, out_specs=out_specs, check_vma=False
    )
```

time: 516 us -> 189 us (0.37)
  the two profiles are of different devices: /device:TPU:1 before, /device:TPU:2 now
where the time goes in v1:
time: 189 us; the launch traced here: 188 us
  blocking collectives  93.1 us (49%)
  waiting for transfers between devices  46 us (24%)
  matrix products  17.1 us (9%)
  between operations  14.3 us (8%)
  local copies, waits for them, and re-layouts  11.5 us (6%)
  other arithmetic  4.15 us (2%)
  starting transfers between devices  1.95 us (1%)
    all_to_all x1, blocking collectives, local(): mine = lax.all_to_all(message, EXPERT_AXES, 0, 0, tiled=True)  52.5 us
    all_to_all x1, blocking collectives, local(): back = lax.all_to_all(reply, EXPERT_AXES, 0, 0, tiled=True)  40.6 us
    ppermute x1, waiting for transfers between devices, local(): other = lax.ppermute(mine, 'xh', [(0, 1), (1, 0)])  36.1 us
    reduce_scatter x1, waiting for transfers between devices, local(): lax.psum_scatter(partial, 'z', scatter_dimension=0, tiled=True)  9.94 us
    dot_general x3, matrix products, dot_t(): lax.dot_general(a, b, (((0,), (0,)), ((), ())), preferred_element_type=jn...  6.93 us
    dot_general x1, matrix products, local(): lax.dot_general(dz_in, matrix, (((1,), (1,)), ((), ())), preferred_elemen...  4.98 us
    dot_general x1, matrix products, local(): z = jnp.dot(x_in, matrix, preferred_element_type=jnp.float32)  4.08 us
  transfers between devices with their start and end apart: 2, of which 2 were waited for; matrix products, arithmetic and copies ran while one was open for 8% of the time, Pallas kernels for 0%

profile of v1, /device:TPU:2, one launch (start us, length us, event | category | flops | bytes accessed | tf_op | source)
XLA Modules:
  0.0 188.1 jit_solution(15644745559009988436)
XLA Ops:
  7.2 0.0 copy-start.2
  7.2 0.0 copy-start.3
  7.2 0.0 copy-start.1
  7.2 0.0 reduce-scatter.2.cloned.1.call-start
  7.2 0.8 copy.52
  8.1 0.1 eq.49
  8.2 0.1 eq.45
  8.3 1.2 reduce-window.6
  9.4 0.2 slice_reduce_fusion
  9.7 0.1 fusion.28
  9.8 0.1 reduce_sum.39
  9.9 0.8 copy.57
  10.7 1.6 convolution_convert_fusion.3
  12.3 0.3 reshape.101
  12.5 0.1 copy.55
  12.6 0.0 copy-done.2
  12.6 0.1 copy.56
  12.7 0.2 convert_reduce_fusion
  12.9 0.0 copy-done.3
  12.9 0.0 copy-done.1
  13.0 0.6 convolution_convert_fusion.1
  13.5 0.6 reshape.99
  14.2 0.1 pad.13.clone
  14.3 0.5 maximum_maximum_fusion
  14.8 52.5 %all_to_all.10 = bf16[32,192,128]{2,1,0:T(8,128)(2,1)S(1)} all-to-all(bf16[32,192,128]{2,1,0:T(8,128)(2,1)S(1)} %maximum_maximum_fusion), channel_id=1, replica_groups=mesh['xh'=2,'z'=12,'y'=8,'xl'=2,'c'=2] {'y','xl','c'}, dimensions={0} | all-to-all | bytes 3145728 | tf_op jit(solution)/shard_map/all_to_all | solution.py:55
  67.2 1.9 %collective-permute-start = (bf16[32,192,128]{2,1,0:T(8,128)(2,1)S(1)}, bf16[32,192,128]{2,1,0:T(8,128)(2,1)}, u32[]{:S(2)}, u32[]{:S(2)}) collective-permute-start(bf16[32,192,128]{2,1,0:T(8,128)(2,1)S(1)} %all_to_all.10), channel_id=1, source_target_pairs={{0,384},{384,0},{1,385},{385,1},{2,386},{386,2},{3,387},{387,3},{4... | collective-permute-start | bytes 4718600 | tf_op jit(solution)/shard_map/ppermute | solution.py:56
  69.2 0.3 reshape.102
  69.4 0.1 slice.34
  69.5 1.4 reshape.104
  71.0 36.1 %collective-permute-done = bf16[32,192,128]{2,1,0:T(8,128)(2,1)} collective-permute-done((bf16[32,192,128]{2,1,0:T(8,128)(2,1)S(1)}, bf16[32,192,128]{2,1,0:T(8,128)(2,1)}, u32[]{:S(2)}, u32[]{:S(2)}) %collective-permute-start) | collective-permute-done | bytes 1572896 | tf_op jit(solution)/shard_map/ppermute | solution.py:56
  107.1 1.0 slice.37
  108.0 0.3 reshape.107
  108.3 1.4 slice.38
  109.8 0.0 copy-start
  109.8 1.4 reshape.108
  111.2 0.0 copy-done
  111.2 4.8 %convolution_convert_fusion = bf16[384,4096]{1,0:T(8,128)(2,1)} fusion(bf16[160,4096]{1,0:T(8,128)(2,1)} %reshape.108, bf16[160,4096]{1,0:T(8,128)(2,1)S(1)} %copy-done, bf16[160,384]{1,0:T(8,128)(2,1)S(1)} %constant_dynamic-slice_fusion, bf16[160,384]{1,0:T(8,128)(2,1)S(1)} %constant_dynamic-slice_fusion.1), kind=kOutput, calls=%fused_computation.4 | convolution fusion | flops 1013940224 | bytes 6012928 | tf_op jit(solution)/shard_map/dot_general | solution.py:13
  116.1 0.0 reduce-scatter.2.cloned.1.call-update
  116.1 4.1 %fusion.15 = bf16[160]{0:T(256)(128)(2,1)S(1)} fusion(bf16[160,4096]{1,0:T(8,128)(2,1)S(1)} %copy-done, bf16[1,4096,768]{2,1,0:T(8,128)(2,1)} %param.11, bf16[160,768]{1,0:T(8,128)(2,1)S(1)} %reshape.102), kind=kOutput, calls=%fused_computation.18 | convolution fusion | flops 1007001472 | bytes 7848256 | tf_op jit(solution)/shard_map/dot_general | solution.py:68
  120.2 0.1 convert_element_type.103
  120.3 5.0 %fusion.4 = bf16[160,4096]{1,0:T(8,128)(2,1)S(1)} fusion(bf16[160,768]{1,0:T(8,128)(2,1)S(1)} %reshape.102, bf16[1,4096,768]{2,1,0:T(8,128)(2,1)} %param.11), kind=kOutput, calls=%fused_computation.5 | convolution fusion | flops 1007288320 | bytes 7847936 | tf_op jit(solution)/shard_map/dot_general | solution.py:65
  125.3 0.6 reshape.103
  125.9 0.1 fusion.11
  126.0 40.6 %all_to_all.11 = bf16[32,176,128]{2,1,0:T(8,128)(2,1)S(1)} all-to-all(bf16[32,176,128]{2,1,0:T(8,128)(2,1)S(1)} %fusion.11), channel_id=1, replica_groups=mesh['xh'=2,'z'=12,'y'=8,'xl'=2,'c'=2] {'y','xl','c'}, dimensions={0} | all-to-all | bytes 2883584 | tf_op jit(solution)/shard_map/all_to_all | solution.py:77
  166.7 0.1 reshape.109
  166.8 0.1 select_reduce_fusion
  166.9 0.1 reshape.106
  167.1 0.7 copy.59
  167.7 0.1 slice.35
  167.8 0.6 reshape.105
  168.4 1.1 convolution_convert_fusion.2
  169.5 9.9 %reduce-scatter.2.cloned.1.call-done = bf16[32,4096]{1,0:T(8,128)(2,1)} async-done(((bf16[384,4096]{1,0:T(8,128)(2,1)}), bf16[32,4096]{1,0:T(8,128)(2,1)}) %reduce-scatter.2.cloned.1.call-update) | async-done | bytes 262160 | tf_op jit(solution)/shard_map/reduce_scatter | solution.py:90
  179.5 1.8 convert_bitcast_fusion
  (13 shorter events, 0.2 us)
Async XLA Ops:
  7.2 5.4 %copy-start.2 = (s32[64,8]{0,1:T(8,128)S(1)}, s32[64,8]{0,1:T(8,128)}, u32[]{:S(2)}) copy-start(s32[64,8]{0,1:T(8,128)} %param.8) | copy-start | bytes 6148
  7.2 5.8 %copy-start.3 = (bf16[64]{0:T(256)(128)(2,1)S(1)}, bf16[64]{0:T(256)(128)(2,1)}, u32[]{:S(2)}) copy-start(bf16[64]{0:T(256)(128)(2,1)} %param.7) | copy-start | bytes 388
  7.2 5.8 %copy-start.1 = (bf16[64,4096]{1,0:T(8,128)(2,1)S(1)}, bf16[64,4096]{1,0:T(8,128)(2,1)}, u32[]{:S(2)}) copy-start(bf16[64,4096]{1,0:T(8,128)(2,1)} %param.6) | copy-start | bytes 1572868
  7.2 172.3 %reduce-scatter.2.cloned.1.call-start = ((), (), s32[]{:S(2)}) async-start(), calls=%async_computation.3 | async-start | bytes 3407872 | tf_op jit(solution)/shard_map/reduce_scatter | solution.py:90
  67.2 39.9 %collective-permute-start = (bf16[32,192,128]{2,1,0:T(8,128)(2,1)S(1)}, bf16[32,192,128]{2,1,0:T(8,128)(2,1)}, u32[]{:S(2)}, u32[]{:S(2)}) collective-permute-start(bf16[32,192,128]{2,1,0:T(8,128)(2,1)S(1)} %all_to_all.10), channel_id=1, source_target_pairs={{0,384},{384,0},{1,385},{385,1},{2,386},{386,2},{3,387},{387,3},{4... | collective-permute-start | bytes 4718600 | tf_op jit(solution)/shard_map/ppermute | solution.py:56
  109.8 1.5 copy-start
Sparse Core Ops, SparseCore 0:
  116.2 63.2 reduce-scatter.1

commit v2 on v1

--- a/solution.py
+++ b/solution.py
@@ -18,6 +18,7 @@
     width = token_rows.shape[1]
     hidden = upstream.shape[2]
     experts = lax.axis_size(EXPERT_AXES)
+    depth = lax.axis_size("z")
     slots = experts * CAP
     choices = toks * picks
     half = hidden // 2
@@ -53,14 +54,17 @@
         axis=1,
     )
     mine = lax.all_to_all(message, EXPERT_AXES, 0, 0, tiled=True)
-    other = lax.ppermute(mine, "xh", [(0, 1), (1, 0)])
+    x_in = mine[:, :x_lines].reshape(slots, width)
+    dz_in = mine[:, x_lines : x_lines + dz_lines].reshape(slots, hidden)
 
-    def unpack(raw):
-        rows = raw[:, :x_lines].reshape(slots, width)
-        grads = raw[:, x_lines : x_lines + dz_lines].reshape(slots, hidden)
-        return rows, grads
+    unit = jnp.arange(hidden)
+    shard = hidden // (2 * depth)
+    source = (unit // shard % 2) * half + unit // (2 * shard) * shard + unit % shard
+    reorder = (unit[:, None] == source[None, :]).astype(jnp.bfloat16)
+    dz_ordered = jnp.dot(dz_in, reorder, preferred_element_type=jnp.float32).astype(jnp.bfloat16)
+    partial = dot_t(dz_ordered, x_in).astype(jnp.bfloat16)
+    summed = lax.psum_scatter(partial, "z", scatter_dimension=0, tiled=True)
 
-    x_in, dz_in = unpack(mine)
     matrix = weight[0]
     row_grads = lax.dot_general(
         dz_in, matrix, (((1,), (1,)), ((), ())), preferred_element_type=jnp.float32
@@ -76,18 +80,11 @@
     )
     back = lax.all_to_all(reply, EXPERT_AXES, 0, 0, tiled=True)
 
-    x_other, dz_other = unpack(other)
-    at = lax.axis_index("xh") * half
-    x_both = jnp.concatenate([x_in, x_other], axis=0)
-    dz_both = jnp.concatenate(
-        [
-            lax.dynamic_slice_in_dim(dz_in, at, half, 1),
-            lax.dynamic_slice_in_dim(dz_other, at, half, 1),
-        ],
-        axis=0,
-    )
-    partial = dot_t(dz_both, x_both).astype(jnp.bfloat16)
-    weight_grads = lax.psum_scatter(partial, "z", scatter_dimension=0, tiled=True)
+    side = lax.axis_index("xh")
+    keep = lax.dynamic_slice_in_dim(summed, side * shard, shard, 0)
+    give = lax.dynamic_slice_in_dim(summed, (1 - side) * shard, shard, 0)
+    got = lax.ppermute(give, "xh", [(0, 1), (1, 0)])
+    weight_grads = keep.astype(jnp.float32) + got.astype(jnp.float32)
 
     back_rows = back[:, :x_lines].reshape(slots, width)
     back_terms = back[:, x_lines, :CAP].reshape(slots).astype(jnp.float32)
@@ -98,7 +95,7 @@
     gate_grads = (picked.reshape(toks, picks) / gate_values.astype(jnp.float32)).astype(
         jnp.bfloat16
     )
-    return token_grads, gate_grads, weight_grads.astype(jnp.float32).T[None]
+    return token_grads, gate_grads, weight_grads.T[None]
 
 
 def solution(mesh):

time: 189 us -> 180 us (0.952)
  the two profiles are of different devices: /device:TPU:2 before, /device:TPU:1 now
where the time goes in v2:
time: 180 us
  waiting for transfers between devices  106 us (59%)
  starting transfers between devices  24 us (13%)
  matrix products  16.8 us (9%)
  between operations  14.3 us (8%)
  local copies, waits for them, and re-layouts  13.2 us (7%)
  other arithmetic  5.5 us (3%)
    all_to_all x1, waiting for transfers between devices, local(): mine = lax.all_to_all(message, EXPERT_AXES, 0, 0, tiled=True)  39.1 us
    all_to_all x1, waiting for transfers between devices, local(): back = lax.all_to_all(reply, EXPERT_AXES, 0, 0, tiled=True)  36.5 us
    reduce_scatter x1, waiting for transfers between devices, local(): summed = lax.psum_scatter(partial, 'z', scatter_dimension=0, tiled=True)  25.4 us
    all_to_all x1, starting transfers between devices, local(): mine = lax.all_to_all(message, EXPERT_AXES, 0, 0, tiled=True)  14.1 us
    dot_general x3, matrix products, dot_t(): lax.dot_general(a, b, (((0,), (0,)), ((), ())), preferred_element_type=jn...  6.59 us
    all_to_all x1, starting transfers between devices, local(): back = lax.all_to_all(reply, EXPERT_AXES, 0, 0, tiled=True)  5.25 us
    dot_general x1, matrix products, local(): lax.dot_general(dz_in, matrix, (((1,), (1,)), ((), ())), preferred_elemen...  4.98 us
    ppermute x1, waiting for transfers between devices, local(): got = lax.ppermute(give, 'xh', [(0, 1), (1, 0)])  4.88 us
  transfers between devices with their start and end apart: 4, of which 4 were waited for; matrix products, arithmetic and copies ran while one was open for 9% of the time, Pallas kernels for 0%

profile of v2, /device:TPU:1, one launch (start us, length us, event | category | flops | bytes accessed | tf_op | source)
XLA Modules:
  0.0 179.7 jit_solution(11024817265342616472)
XLA Ops:
  7.2 0.0 copy-start.2
  7.2 0.0 copy-start.3
  7.2 0.0 copy-start.1
  7.2 0.8 copy.52
  8.0 0.1 eq.61
  8.1 0.1 eq.65
  8.2 1.2 reduce-window.6
  9.4 0.2 slice_reduce_fusion
  9.7 0.1 fusion.25
  9.8 0.1 reduce_sum.39
  9.9 0.8 copy.57
  10.7 1.6 convolution_convert_fusion.3
  12.2 0.3 reshape.138
  12.5 0.0 copy-done.3
  12.5 0.1 copy.55
  12.6 0.0 copy-done.2
  12.6 0.1 copy.56
  12.7 0.2 convert_reduce_fusion
  12.9 0.0 copy-done.1
  12.9 0.6 convolution_convert_fusion.1
  13.5 0.6 reshape.136
  14.1 0.1 pad.9.clone
  14.2 1.7 maximum_maximum_fusion
  15.9 14.1 %all-to-all-start = ((bf16[32,192,128]{2,1,0:T(8,128)(2,1)}), bf16[32,192,128]{2,1,0:T(8,128)(2,1)S(1)}, u32[]{:S(2)}, u32[]{:S(2)}) async-start(bf16[32,192,128]{2,1,0:T(8,128)(2,1)} %maximum_maximum_fusion), calls=%async_computation | async-start | bytes 3145728 | tf_op jit(solution)/shard_map/all_to_all | solution.py:56
  30.0 0.0 reduce-scatter.2.cloned.1.call-start
  30.1 39.1 %all-to-all-done = bf16[32,192,128]{2,1,0:T(8,128)(2,1)S(1)} async-done(((bf16[32,192,128]{2,1,0:T(8,128)(2,1)}), bf16[32,192,128]{2,1,0:T(8,128)(2,1)S(1)}, u32[]{:S(2)}, u32[]{:S(2)}) %all-to-all-start) | async-done | bytes 1572896 | tf_op jit(solution)/shard_map/all_to_all | solution.py:56
  69.2 1.1 slice.26
  70.4 2.4 %reshape.141 = bf16[160,4096]{1,0:T(8,128)(2,1)S(1)} reshape(bf16[32,160,128]{2,1,0:T(8,128)(2,1)} %slice.26) | data formatting | bytes 2621440 | tf_op jit(solution)/shard_map/reshape | solution.py:57
  72.8 0.3 reshape.139
  73.0 4.5 %convolution_convert_fusion = bf16[768,4096]{1,0:T(8,128)(2,1)} fusion(bf16[160,4096]{1,0:T(8,128)(2,1)S(1)} %reshape.141, bf16[160,768]{1,0:T(8,128)(2,1)S(1)} %reshape.139, s32[768]{0:T(1024)S(1)} %fusion.39), kind=kOutput, calls=%fused_computation | convolution fusion | flops 1199235072 | bytes 7851008 | tf_op jit(solution)/shard_map/dot_general | solution.py:13
  77.5 0.0 reduce-scatter.2.cloned.1.call-update
  77.5 4.1 %fusion.15 = bf16[160]{0:T(256)(128)(2,1)S(1)} fusion(bf16[160,4096]{1,0:T(8,128)(2,1)S(1)} %reshape.141, bf16[1,4096,768]{2,1,0:T(8,128)(2,1)} %param.11, bf16[160,768]{1,0:T(8,128)(2,1)S(1)} %reshape.139), kind=kOutput, calls=%fused_computation.19 | convolution fusion | flops 1007001472 | bytes 7848256 | tf_op jit(solution)/shard_map/dot_general | solution.py:72
  81.6 0.1 convert_element_type.115
  81.7 5.0 %fusion.4 = bf16[160,4096]{1,0:T(8,128)(2,1)S(1)} fusion(bf16[160,768]{1,0:T(8,128)(2,1)S(1)} %reshape.139, bf16[1,4096,768]{2,1,0:T(8,128)(2,1)} %param.11), kind=kOutput, calls=%fused_computation.5 | convolution fusion | flops 1007288320 | bytes 7847936 | tf_op jit(solution)/shard_map/dot_general | solution.py:69
  86.7 0.6 reshape.140
  87.4 1.2 fusion.9
  88.6 5.2 %all-to-all-start.1 = ((bf16[32,176,128]{2,1,0:T(8,128)(2,1)}), bf16[32,176,128]{2,1,0:T(8,128)(2,1)S(1)}, u32[]{:S(2)}, u32[]{:S(2)}) async-start(bf16[32,176,128]{2,1,0:T(8,128)(2,1)} %fusion.9), calls=%async_computation.1 | async-start | bytes 2883584 | tf_op jit(solution)/shard_map/all_to_all | solution.py:81
  93.9 36.5 %all-to-all-done.1 = bf16[32,176,128]{2,1,0:T(8,128)(2,1)S(1)} async-done(((bf16[32,176,128]{2,1,0:T(8,128)(2,1)}), bf16[32,176,128]{2,1,0:T(8,128)(2,1)S(1)}, u32[]{:S(2)}, u32[]{:S(2)}) %all-to-all-start.1) | async-done | bytes 1441824 | tf_op jit(solution)/shard_map/all_to_all | solution.py:81
  130.3 1.2 slice.27
  131.5 2.4 %reshape.142 = bf16[160,4096]{1,0:T(8,128)(2,1)S(1)} reshape(bf16[32,160,128]{2,1,0:T(8,128)(2,1)} %slice.27) | data formatting | bytes 2621440 | tf_op jit(solution)/shard_map/reshape | solution.py:89
  133.9 0.1 reshape.144
  134.0 0.1 select_reduce_fusion
  134.2 0.1 reshape.143
  134.3 0.7 copy.59
  134.9 25.4 %reduce-scatter.2.cloned.1.call-done = bf16[64,4096]{1,0:T(8,128)(2,1)} async-done(((bf16[768,4096]{1,0:T(8,128)(2,1)}), bf16[64,4096]{1,0:T(8,128)(2,1)}) %reduce-scatter.2.cloned.1.call-update) | async-done | bytes 524304 | tf_op jit(solution)/shard_map/reduce_scatter | solution.py:66
  160.4 0.0 copy-start
  160.4 1.0 constant_dynamic-slice_fusion
  161.4 4.6 %collective-permute-start = (bf16[32,4096]{1,0:T(8,128)(2,1)S(1)}, bf16[32,4096]{1,0:T(8,128)(2,1)S(1)}, u32[]{:S(2)}, u32[]{:S(2)}) collective-permute-start(bf16[32,4096]{1,0:T(8,128)(2,1)S(1)} %constant_dynamic-slice_fusion), channel_id=1, source_target_pairs={{0,384},{384,0},{1,385},{385,1},{2,386},{386,2},{3,387},{387,3},{4... | collective-permute-start | bytes 786440 | tf_op jit(solution)/shard_map/ppermute | solution.py:86
  166.0 1.1 convolution_convert_fusion.2
  167.2 4.9 %collective-permute-done = bf16[32,4096]{1,0:T(8,128)(2,1)S(1)} collective-permute-done((bf16[32,4096]{1,0:T(8,128)(2,1)S(1)}, bf16[32,4096]{1,0:T(8,128)(2,1)S(1)}, u32[]{:S(2)}, u32[]{:S(2)}) %collective-permute-start) | collective-permute-done | bytes 262176 | tf_op jit(solution)/shard_map/ppermute | solution.py:86
  172.0 0.0 copy-done
  172.0 0.8 add_bitcast_fusion
  (12 shorter events, 0.2 us)
Async XLA Ops:
  7.2 5.4 %copy-start.2 = (s32[64,8]{0,1:T(8,128)S(1)}, s32[64,8]{0,1:T(8,128)}, u32[]{:S(2)}) copy-start(s32[64,8]{0,1:T(8,128)} %param.8) | copy-start | bytes 6148
  7.2 5.3 %copy-start.3 = (bf16[64]{0:T(256)(128)(2,1)S(1)}, bf16[64]{0:T(256)(128)(2,1)}, u32[]{:S(2)}) copy-start(bf16[64]{0:T(256)(128)(2,1)} %param.7) | copy-start | bytes 388
  7.2 5.7 %copy-start.1 = (bf16[64,4096]{1,0:T(8,128)(2,1)S(1)}, bf16[64,4096]{1,0:T(8,128)(2,1)}, u32[]{:S(2)}) copy-start(bf16[64,4096]{1,0:T(8,128)(2,1)} %param.6) | copy-start | bytes 1572868
  15.9 53.3 %all-to-all-start = ((bf16[32,192,128]{2,1,0:T(8,128)(2,1)}), bf16[32,192,128]{2,1,0:T(8,128)(2,1)S(1)}, u32[]{:S(2)}, u32[]{:S(2)}) async-start(bf16[32,192,128]{2,1,0:T(8,128)(2,1)} %maximum_maximum_fusion), calls=%async_computation | async-start | bytes 3145728 | tf_op jit(solution)/shard_map/all_to_all | solution.py:56
  30.0 130.3 %reduce-scatter.2.cloned.1.call-start = ((), (), s32[]{:S(2)}) async-start(), calls=%async_computation.3 | async-start | bytes 6815744 | tf_op jit(solution)/shard_map/reduce_scatter | solution.py:66
  88.6 41.7 %all-to-all-start.1 = ((bf16[32,176,128]{2,1,0:T(8,128)(2,1)}), bf16[32,176,128]{2,1,0:T(8,128)(2,1)S(1)}, u32[]{:S(2)}, u32[]{:S(2)}) async-start(bf16[32,176,128]{2,1,0:T(8,128)(2,1)} %fusion.9), calls=%async_computation.1 | async-start | bytes 2883584 | tf_op jit(solution)/shard_map/all_to_all | solution.py:81
  160.4 11.7 %copy-start = (bf16[64,4096]{1,0:T(8,128)(2,1)S(1)}, bf16[64,4096]{1,0:T(8,128)(2,1)}, u32[]{:S(2)}) copy-start(bf16[64,4096]{1,0:T(8,128)(2,1)} %reduce-scatter.2.cloned.1.call-done) | copy-start | bytes 1572868
  161.4 10.6 %collective-permute-start = (bf16[32,4096]{1,0:T(8,128)(2,1)S(1)}, bf16[32,4096]{1,0:T(8,128)(2,1)S(1)}, u32[]{:S(2)}, u32[]{:S(2)}) collective-permute-start(bf16[32,4096]{1,0:T(8,128)(2,1)S(1)} %constant_dynamic-slice_fusion), channel_id=1, source_target_pairs={{0,384},{384,0},{1,385},{385,1},{2,386},{386,2},{3,387},{387,3},{4... | collective-permute-start | bytes 786440 | tf_op jit(solution)/shard_map/ppermute | solution.py:86
Sparse Core Ops, SparseCore 0:
  77.6 82.6 reduce-scatter.1

commit v3 on v2

--- a/solution.py
+++ b/solution.py
@@ -1,6 +1,8 @@
 import jax
 import jax.numpy as jnp
 from jax import lax
+from jax.experimental import pallas as pl
+from jax.experimental.pallas import tpu as pltpu
 from jax.sharding import Mesh, PartitionSpec as P
 
 CAP = 5
@@ -11,6 +13,41 @@
 
 def dot_t(a, b):
     return lax.dot_general(a, b, (((0,), (0,)), ((), ())), preferred_element_type=jnp.float32)
+
+
+def partial_kernel(x_ref, dz_ref, order_ref, out_ref, dz_t):
+    @pl.when(pl.program_id(0) == 0)
+    def _():
+        dz_t[...] = lax.dot_general(
+            order_ref[...], dz_ref[...], (((0,), (1,)), ((), ())), preferred_element_type=jnp.float32
+        ).astype(jnp.bfloat16)
+
+    out_ref[...] = jnp.dot(
+        dz_t[...], x_ref[...], preferred_element_type=jnp.float32
+    ).astype(jnp.bfloat16)
+
+
+def partial_of(x, dz, order, block=512):
+    rows, width = x.shape
+    hidden = dz.shape[1]
+    return pl.pallas_call(
+        partial_kernel,
+        grid=(width // block,),
+        in_specs=[
+            pl.BlockSpec((rows, block), lambda i: (0, i)),
+            pl.BlockSpec((rows, hidden), lambda i: (0, 0)),
+            pl.BlockSpec((hidden, hidden), lambda i: (0, 0)),
+        ],
+        out_specs=pl.BlockSpec((hidden, block), lambda i: (0, i)),
+        out_shape=jax.ShapeDtypeStruct((hidden, width), jnp.bfloat16),
+        scratch_shapes=[pltpu.VMEM((hidden, rows), jnp.bfloat16)],
+        compiler_params=pltpu.CompilerParams(vmem_limit_bytes=16 * 1024 * 1024),
+        cost_estimate=pl.CostEstimate(
+            flops=2 * rows * hidden * (width + hidden),
+            bytes_accessed=2 * (hidden * width + rows * width + hidden * hidden),
+            transcendentals=0,
+        ),
+    )(x, dz, order)
 
 
 def local(token_rows, row_scales, expert_ids, gate_values, upstream, weight):
@@ -31,20 +68,20 @@
     dz = (gate_values.astype(jnp.float32)[..., None] * upstream.astype(jnp.float32)).astype(
         jnp.bfloat16
     )
-    ids = expert_ids.reshape(choices)
-    onehot = (ids[:, None] == jnp.arange(experts, dtype=jnp.int32)[None, :]).astype(jnp.int32)
-    before = jnp.cumsum(onehot, axis=0) - onehot
-    slot = jnp.sum(before * onehot, axis=1)
-    position = jnp.where(ids < experts, ids * CAP + slot, -1)
-    placing = position[:, None] == jnp.arange(slots, dtype=jnp.int32)[None, :]
+    column = jnp.arange(slots, dtype=jnp.int32)
+    named = expert_ids[:, :, None] == (column // CAP)[None, None, :]
+    names = jnp.any(named, axis=1)
+    row = jnp.arange(toks, dtype=jnp.int32)
+    earlier = (row[None, :] < row[:, None]).astype(jnp.bfloat16)
+    rank = jnp.dot(earlier, names.astype(jnp.bfloat16), preferred_element_type=jnp.float32)
+    token_placing = names & (rank == (column % CAP).astype(jnp.float32)[None, :])
+    token_place = token_placing.astype(jnp.bfloat16)
+    placing = (named & token_placing[:, None, :]).reshape(choices, slots)
     place = placing.astype(jnp.bfloat16)
-    token_place = jnp.sum(
-        placing.astype(jnp.int32).reshape(toks, picks, slots), axis=1
-    ).astype(jnp.bfloat16)
 
     send_x = dot_t(token_place, x).astype(jnp.bfloat16)
     send_dz = dot_t(place, dz.reshape(choices, hidden)).astype(jnp.bfloat16)
-    pad = (-(x_lines + dz_lines)) % 16
+    pad = width // LANE - dz_lines
     message = jnp.concatenate(
         [
             send_x.reshape(experts, x_lines, LANE),
@@ -54,15 +91,17 @@
         axis=1,
     )
     mine = lax.all_to_all(message, EXPERT_AXES, 0, 0, tiled=True)
-    x_in = mine[:, :x_lines].reshape(slots, width)
+    x_in = mine.reshape(experts * (CAP + 1), width)
     dz_in = mine[:, x_lines : x_lines + dz_lines].reshape(slots, hidden)
+    dz_six = jnp.pad(dz_in.reshape(experts, CAP, hidden), ((0, 0), (0, 1), (0, 0))).reshape(
+        experts * (CAP + 1), hidden
+    )
 
     unit = jnp.arange(hidden)
     shard = hidden // (2 * depth)
     source = (unit // shard % 2) * half + unit // (2 * shard) * shard + unit % shard
     reorder = (unit[:, None] == source[None, :]).astype(jnp.bfloat16)
-    dz_ordered = jnp.dot(dz_in, reorder, preferred_element_type=jnp.float32).astype(jnp.bfloat16)
-    partial = dot_t(dz_ordered, x_in).astype(jnp.bfloat16)
+    partial = partial_of(x_in, dz_six, reorder)
     summed = lax.psum_scatter(partial, "z", scatter_dimension=0, tiled=True)
 
     matrix = weight[0]
@@ -70,7 +109,8 @@
         dz_in, matrix, (((1,), (1,)), ((), ())), preferred_element_type=jnp.float32
     ).astype(jnp.bfloat16)
     z = jnp.dot(x_in, matrix, preferred_element_type=jnp.float32)
-    terms = jnp.sum(dz_in.astype(jnp.float32) * z, axis=1).astype(jnp.bfloat16)
+    terms = jnp.sum(dz_six.astype(jnp.float32) * z, axis=1).astype(jnp.bfloat16)
+    terms = terms.reshape(experts, CAP + 1)[:, :CAP]
     reply = jnp.concatenate(
         [
             row_grads.reshape(experts, x_lines, LANE),

time: 180 us -> 184 us (1.022)
  matrix products: 16.8 us -> 11.5 us
  Pallas kernels: 0 us -> 3.95 us
  waiting for transfers between devices: 106 us -> 108 us
    dot_general x3 -> x2, matrix products: 6.59 us -> 1.02 us  [dot_t(): lax.dot_general(a, b, (((0,), (0,)), ((), ())), preferred_element_type=jn...]
    pallas_call x0 -> x1, Pallas kernels: none -> 3.95 us  [partial_of(): pl.pallas_call(partial_kernel, grid=(width // block,), in_specs=[pl.Block...]
    reduce_scatter x1, waiting for transfers between devices: 25.4 us -> 27.6 us  [local(): summed = lax.psum_scatter(partial, 'z', scatter_dimension=0, tiled=True)]
  transfers between devices with their start and end apart: 4 -> 4, of which waited for: 4 -> 4; matrix products, arithmetic and copies ran while one was open for 9% -> 8% of each run, Pallas kernels for 0% -> 0%
where the time goes in v3:
time: 184 us; the launch traced here: 183 us
  waiting for transfers between devices  108 us (59%)
  starting transfers between devices  24.1 us (13%)
  local copies, waits for them, and re-layouts  14.5 us (8%)
  between operations  14.3 us (8%)
  matrix products  11.5 us (6%)
  other arithmetic  7.24 us (4%)
  Pallas kernels  3.95 us (2%)
    all_to_all x1, waiting for transfers between devices, local(): mine = lax.all_to_all(message, EXPERT_AXES, 0, 0, tiled=True)  38.7 us
    all_to_all x1, waiting for transfers between devices, local(): back = lax.all_to_all(reply, EXPERT_AXES, 0, 0, tiled=True)  36.5 us
    reduce_scatter x1, waiting for transfers between devices, local(): summed = lax.psum_scatter(partial, 'z', scatter_dimension=0, tiled=True)  27.6 us
    all_to_all x1, starting transfers between devices, local(): mine = lax.all_to_all(message, EXPERT_AXES, 0, 0, tiled=True)  14.1 us
    all_to_all x1, starting transfers between devices, local(): back = lax.all_to_all(reply, EXPERT_AXES, 0, 0, tiled=True)  5.26 us
    dot_general x1, matrix products, local(): lax.dot_general(dz_in, matrix, (((1,), (1,)), ((), ())), preferred_elemen...  4.98 us
    ppermute x1, waiting for transfers between devices, local(): got = lax.ppermute(give, 'xh', [(0, 1), (1, 0)])  4.87 us
    ppermute x1, starting transfers between devices, local(): got = lax.ppermute(give, 'xh', [(0, 1), (1, 0)])  4.61 us
  transfers between devices with their start and end apart: 4, of which 4 were waited for; matrix products, arithmetic and copies ran while one was open for 8% of the time, Pallas kernels for 0%

profile of v3, /device:TPU:1, one launch (start us, length us, event | category | flops | bytes accessed | tf_op | source)
XLA Modules:
  0.0 183.3 jit_solution(12780462643552547553)
XLA Ops:
  7.2 0.0 copy-start.4
  7.2 0.8 copy.22
  8.0 0.8 compare_reduce_fusion
  8.8 0.1 fusion.17
  8.9 1.3 multiply_convert_fusion
  10.3 0.0 copy-done.4
  10.3 0.0 copy-start.6
  10.3 0.0 copy-start.3
  10.3 0.5 fusion.13
  10.8 0.3 reshape.133
  11.0 0.0 copy-done.6
  11.1 0.3 copy-done.3
  11.4 0.6 convolution_convert_fusion
  11.9 0.6 reshape.132
  12.6 0.1 pad.14.clone
  12.7 1.7 maximum_maximum_fusion
  14.3 14.1 %all-to-all-start = ((bf16[32,192,128]{2,1,0:T(8,128)(2,1)}), bf16[32,192,128]{2,1,0:T(8,128)(2,1)S(1)}, u32[]{:S(2)}, u32[]{:S(2)}) async-start(bf16[32,192,128]{2,1,0:T(8,128)(2,1)} %maximum_maximum_fusion), calls=%async_computation | async-start | bytes 3145728 | tf_op jit(solution)/shard_map/all_to_all | solution.py:93
  28.5 0.0 reduce-scatter.2.cloned.1.call-start
  28.5 0.4 fusion.8.order_ref
  29.0 38.7 %all-to-all-done = bf16[32,192,128]{2,1,0:T(8,128)(2,1)S(1)} async-done(((bf16[32,192,128]{2,1,0:T(8,128)(2,1)}), bf16[32,192,128]{2,1,0:T(8,128)(2,1)S(1)}, u32[]{:S(2)}, u32[]{:S(2)}) %all-to-all-start) | async-done | bytes 1572896 | tf_op jit(solution)/shard_map/all_to_all | solution.py:93
  67.7 0.0 copy-start.1
  67.7 1.2 reshape_reshape.3
  68.9 0.1 copy-done.1
  69.0 1.8 pad.8
  70.8 1.1 reshape.136.dz_ref
  71.9 2.5 %reshape.137.x_ref = bf16[192,4096]{1,0:T(8,128)(2,1)S(1)} reshape(bf16[32,192,128]{2,1,0:T(8,128)(2,1)} %copy-done.1) | data formatting | bytes 3145728 | tf_op jit(solution)/shard_map/reshape | solution.py:94
  74.4 3.9 %shard_map.85 = bf16[768,4096]{1,0:T(8,128)(2,1)S(1)} custom-call(bf16[192,4096]{1,0:T(8,128)(2,1)S(1)} %reshape.137.x_ref, bf16[192,768]{1,0:T(8,128)(2,1)S(1)} %reshape.136.dz_ref, bf16[768,768]{1,0:T(8,128)(2,1)S(1)} %fusion.8.order_ref), custom_call_target="tpu_custom_call" | custom-call | flops 1434451968 | bytes 9043968 | tf_op jit(solution)/shard_map/pallas_call | solution.py:33
  78.4 0.0 copy-start
  78.4 2.6 %copy-done = bf16[768,4096]{1,0:T(8,128)(2,1)} copy-done((bf16[768,4096]{1,0:T(8,128)(2,1)}, bf16[768,4096]{1,0:T(8,128)(2,1)S(1)}, u32[]{:S(2)}) %copy-start) | copy-done | bytes 6291480
  81.0 0.0 reduce-scatter.2.cloned.1.call-update
  81.1 0.3 reshape.134
  81.3 4.3 %fusion.14 = bf16[192]{0:T(256)(128)(2,1)S(1)} fusion(bf16[192,4096]{1,0:T(8,128)(2,1)S(1)} %reshape.137.x_ref, bf16[1,4096,768]{2,1,0:T(8,128)(2,1)} %param.11, bf16[192,768]{1,0:T(8,128)(2,1)S(1)} %reshape.136.dz_ref), kind=kOutput, calls=%fused_computation.17 | convolution fusion | flops 1208401664 | bytes 8159616 | tf_op jit(solution)/shard_map/dot_general | solution.py:111
  85.6 0.1 convert_element_type.90
  85.7 0.1 copy.24
  85.8 0.1 copy.26
  85.9 5.0 %fusion.4 = bf16[160,4096]{1,0:T(8,128)(2,1)S(1)} fusion(bf16[160,768]{1,0:T(8,128)(2,1)S(1)} %reshape.134, bf16[1,4096,768]{2,1,0:T(8,128)(2,1)} %param.11), kind=kOutput, calls=%fused_computation.4 | convolution fusion | flops 1007288320 | bytes 7847936 | tf_op jit(solution)/shard_map/dot_general | solution.py:108
  90.9 0.6 reshape.135
  91.6 1.2 fusion.9
  92.8 5.3 %all-to-all-start.1 = ((bf16[32,176,128]{2,1,0:T(8,128)(2,1)}), bf16[32,176,128]{2,1,0:T(8,128)(2,1)S(1)}, u32[]{:S(2)}, u32[]{:S(2)}) async-start(bf16[32,176,128]{2,1,0:T(8,128)(2,1)} %fusion.9), calls=%async_computation.1 | async-start | bytes 2883584 | tf_op jit(solution)/shard_map/all_to_all | solution.py:121
  98.1 36.5 %all-to-all-done.1 = bf16[32,176,128]{2,1,0:T(8,128)(2,1)S(1)} async-done(((bf16[32,176,128]{2,1,0:T(8,128)(2,1)}), bf16[32,176,128]{2,1,0:T(8,128)(2,1)S(1)}, u32[]{:S(2)}, u32[]{:S(2)}) %all-to-all-start.1) | async-done | bytes 1441824 | tf_op jit(solution)/shard_map/all_to_all | solution.py:121
  134.6 0.1 reshape.140
  134.7 0.1 slice.18
  134.8 0.0 copy-start.5
  134.8 0.6 reshape.139
  135.4 0.3 fusion.20
  135.7 0.0 copy-done.5
  135.7 0.6 divide_convert_fusion
  136.3 27.6 %reduce-scatter.2.cloned.1.call-done = bf16[64,4096]{1,0:T(8,128)(2,1)} async-done(((bf16[768,4096]{1,0:T(8,128)(2,1)}), bf16[64,4096]{1,0:T(8,128)(2,1)}) %reduce-scatter.2.cloned.1.call-update) | async-done | bytes 524304 | tf_op jit(solution)/shard_map/reduce_scatter | solution.py:105
  163.9 0.0 copy-start.2
  163.9 1.0 constant_dynamic-slice_fusion
  165.0 4.6 %collective-permute-start = (bf16[32,4096]{1,0:T(8,128)(2,1)S(1)}, bf16[32,4096]{1,0:T(8,128)(2,1)S(1)}, u32[]{:S(2)}, u32[]{:S(2)}) collective-permute-start(bf16[32,4096]{1,0:T(8,128)(2,1)S(1)} %constant_dynamic-slice_fusion), channel_id=1, source_target_pairs={{0,384},{384,0},{1,385},{385,1},{2,386},{386,2},{3,387},{387,3},{4... | collective-permute-start | bytes 786440 | tf_op jit(solution)/shard_map/ppermute | solution.py:126
  169.6 1.1 convolution_convert_fusion.1
  170.7 4.9 %collective-permute-done = bf16[32,4096]{1,0:T(8,128)(2,1)S(1)} collective-permute-done((bf16[32,4096]{1,0:T(8,128)(2,1)S(1)}, bf16[32,4096]{1,0:T(8,128)(2,1)S(1)}, u32[]{:S(2)}, u32[]{:S(2)}) %collective-permute-start) | collective-permute-done | bytes 262176 | tf_op jit(solution)/shard_map/ppermute | solution.py:126
  175.6 0.0 copy-done.2
  175.6 0.8 add_bitcast_fusion
  (7 shorter events, 0.1 us)
Async XLA Ops:
  7.2 3.1 %copy-start.4 = (s32[64,8]{0,1:T(8,128)S(1)}, s32[64,8]{0,1:T(8,128)}, u32[]{:S(2)}) copy-start(s32[64,8]{0,1:T(8,128)} %param.8) | copy-start | bytes 6148
  10.3 0.8 copy-start.6
  10.3 1.0 copy-start.3
  14.3 53.3 %all-to-all-start = ((bf16[32,192,128]{2,1,0:T(8,128)(2,1)}), bf16[32,192,128]{2,1,0:T(8,128)(2,1)S(1)}, u32[]{:S(2)}, u32[]{:S(2)}) async-start(bf16[32,192,128]{2,1,0:T(8,128)(2,1)} %maximum_maximum_fusion), calls=%async_computation | async-start | bytes 3145728 | tf_op jit(solution)/shard_map/all_to_all | solution.py:93
  28.5 135.4 %reduce-scatter.2.cloned.1.call-start = ((), (), s32[]{:S(2)}) async-start(), calls=%async_computation.3 | async-start | bytes 6815744 | tf_op jit(solution)/shard_map/reduce_scatter | solution.py:105
  67.7 1.3 copy-start.1
  78.4 2.7 %copy-start = (bf16[768,4096]{1,0:T(8,128)(2,1)}, bf16[768,4096]{1,0:T(8,128)(2,1)S(1)}, u32[]{:S(2)}) copy-start(bf16[768,4096]{1,0:T(8,128)(2,1)S(1)} %shard_map.85) | copy-start | bytes 18874372
  92.8 41.8 %all-to-all-start.1 = ((bf16[32,176,128]{2,1,0:T(8,128)(2,1)}), bf16[32,176,128]{2,1,0:T(8,128)(2,1)S(1)}, u32[]{:S(2)}, u32[]{:S(2)}) async-start(bf16[32,176,128]{2,1,0:T(8,128)(2,1)} %fusion.9), calls=%async_computation.1 | async-start | bytes 2883584 | tf_op jit(solution)/shard_map/all_to_all | solution.py:121
  134.8 0.9 copy-start.5
  163.9 11.7 %copy-start.2 = (bf16[64,4096]{1,0:T(8,128)(2,1)S(1)}, bf16[64,4096]{1,0:T(8,128)(2,1)}, u32[]{:S(2)}) copy-start(bf16[64,4096]{1,0:T(8,128)(2,1)} %reduce-scatter.2.cloned.1.call-done) | copy-start | bytes 1572868
  165.0 10.6 %collective-permute-start = (bf16[32,4096]{1,0:T(8,128)(2,1)S(1)}, bf16[32,4096]{1,0:T(8,128)(2,1)S(1)}, u32[]{:S(2)}, u32[]{:S(2)}) collective-permute-start(bf16[32,4096]{1,0:T(8,128)(2,1)S(1)} %constant_dynamic-slice_fusion), channel_id=1, source_target_pairs={{0,384},{384,0},{1,385},{385,1},{2,386},{386,2},{3,387},{387,3},{4... | collective-permute-start | bytes 786440 | tf_op jit(solution)/shard_map/ppermute | solution.py:126
Sparse Core Ops, SparseCore 0:
  81.2 82.6 reduce-scatter.1

commit v4 on v3

--- a/solution.py
+++ b/solution.py
@@ -15,31 +15,31 @@
     return lax.dot_general(a, b, (((0,), (0,)), ((), ())), preferred_element_type=jnp.float32)
 
 
-def partial_kernel(x_ref, dz_ref, order_ref, out_ref, dz_t):
+def partial_kernel(x_ref, dz_ref, order_ref, spread_ref, out_ref, dz_t):
     @pl.when(pl.program_id(0) == 0)
     def _():
-        dz_t[...] = lax.dot_general(
-            order_ref[...], dz_ref[...], (((0,), (1,)), ((), ())), preferred_element_type=jnp.float32
-        ).astype(jnp.bfloat16)
+        ordered = jnp.dot(dz_ref[...], order_ref[...], preferred_element_type=jnp.float32)
+        dz_t[...] = dot_t(ordered.astype(jnp.bfloat16), spread_ref[...]).astype(jnp.bfloat16)
 
     out_ref[...] = jnp.dot(
         dz_t[...], x_ref[...], preferred_element_type=jnp.float32
     ).astype(jnp.bfloat16)
 
 
-def partial_of(x, dz, order, block=512):
+def partial_of(x, dz, order, spread, block=512):
     rows, width = x.shape
-    hidden = dz.shape[1]
+    slots, hidden = dz.shape
     return pl.pallas_call(
         partial_kernel,
         grid=(width // block,),
         in_specs=[
             pl.BlockSpec((rows, block), lambda i: (0, i)),
-            pl.BlockSpec((rows, hidden), lambda i: (0, 0)),
+            pl.BlockSpec((slots, hidden), lambda i: (0, 0)),
             pl.BlockSpec((hidden, hidden), lambda i: (0, 0)),
+            pl.BlockSpec((slots, rows), lambda i: (0, 0)),
         ],
         out_specs=pl.BlockSpec((hidden, block), lambda i: (0, i)),
-        out_shape=jax.ShapeDtypeStruct((hidden, width), jnp.bfloat16),
+        out_shape=pltpu.HBM((hidden, width), jnp.bfloat16),
         scratch_shapes=[pltpu.VMEM((hidden, rows), jnp.bfloat16)],
         compiler_params=pltpu.CompilerParams(vmem_limit_bytes=16 * 1024 * 1024),
         cost_estimate=pl.CostEstimate(
@@ -47,7 +47,7 @@
             bytes_accessed=2 * (hidden * width + rows * width + hidden * hidden),
             transcendentals=0,
         ),
-    )(x, dz, order)
+    )(x, dz, order, spread)
 
 
 def local(token_rows, row_scales, expert_ids, gate_values, upstream, weight):
@@ -93,15 +93,14 @@
     mine = lax.all_to_all(message, EXPERT_AXES, 0, 0, tiled=True)
     x_in = mine.reshape(experts * (CAP + 1), width)
     dz_in = mine[:, x_lines : x_lines + dz_lines].reshape(slots, hidden)
-    dz_six = jnp.pad(dz_in.reshape(experts, CAP, hidden), ((0, 0), (0, 1), (0, 0))).reshape(
-        experts * (CAP + 1), hidden
-    )
 
     unit = jnp.arange(hidden)
     shard = hidden // (2 * depth)
     source = (unit // shard % 2) * half + unit // (2 * shard) * shard + unit % shard
     reorder = (unit[:, None] == source[None, :]).astype(jnp.bfloat16)
-    partial = partial_of(x_in, dz_six, reorder)
+    six = jnp.arange(experts * (CAP + 1))
+    spread = (column + column // CAP)[:, None] == six[None, :]
+    partial = partial_of(x_in, dz_in, reorder, spread.astype(jnp.bfloat16))
     summed = lax.psum_scatter(partial, "z", scatter_dimension=0, tiled=True)
 
     matrix = weight[0]
@@ -109,8 +108,8 @@
         dz_in, matrix, (((1,), (1,)), ((), ())), preferred_element_type=jnp.float32
     ).astype(jnp.bfloat16)
     z = jnp.dot(x_in, matrix, preferred_element_type=jnp.float32)
-    terms = jnp.sum(dz_six.astype(jnp.float32) * z, axis=1).astype(jnp.bfloat16)
-    terms = terms.reshape(experts, CAP + 1)[:, :CAP]
+    z = z.reshape(experts, CAP + 1, hidden)[:, :CAP].reshape(slots, hidden)
+    terms = jnp.sum(dz_in.astype(jnp.float32) * z, axis=1).astype(jnp.bfloat16)
     reply = jnp.concatenate(
         [
             row_grads.reshape(experts, x_lines, LANE),

time: 184 us -> 181 us (0.984)
  waiting for transfers between devices: 108 us -> 99.7 us
  Pallas kernels: 3.95 us -> 6.53 us
    reduce_scatter x1, waiting for transfers between devices: 27.6 us -> 19.7 us  [local(): summed = lax.psum_scatter(partial, 'z', scatter_dimension=0, tiled=True)]
    slice x0 -> x1, matrix products: none -> 5.59 us  [local(): z = z.reshape(experts, CAP + 1, hidden)[:, :CAP].reshape(slots, hidden)]
    dot_general x1 -> x0, matrix products: 4.27 us -> none  [local(): z = jnp.dot(x_in, matrix, preferred_element_type=jnp.float32)]
    dot_general x0 -> x1, local copies, waits for them, and re-layouts: none -> 2.66 us  [local(): z = jnp.dot(x_in, matrix, preferred_element_type=jnp.float32)]
    pallas_call x1, Pallas kernels: 3.95 us -> 6.53 us  [partial_of(): pl.pallas_call(partial_kernel, grid=(width // block,), in_specs=[pl.Block...]
  transfers between devices with their start and end apart: 4 -> 4, of which waited for: 4 -> 4; matrix products, arithmetic and copies ran while one was open for 8% -> 12% of each run, Pallas kernels for 0% -> 0%
where the time goes in v4:
time: 181 us
  waiting for transfers between devices  99.7 us (55%)
  starting transfers between devices  24 us (13%)
  local copies, waits for them, and re-layouts  14.8 us (8%)
  between operations  14.3 us (8%)
  matrix products  12.9 us (7%)
  other arithmetic  8.35 us (5%)
  Pallas kernels  6.53 us (4%)
    all_to_all x1, waiting for transfers between devices, local(): mine = lax.all_to_all(message, EXPERT_AXES, 0, 0, tiled=True)  38.6 us
    all_to_all x1, waiting for transfers between devices, local(): back = lax.all_to_all(reply, EXPERT_AXES, 0, 0, tiled=True)  36.5 us
    reduce_scatter x1, waiting for transfers between devices, local(): summed = lax.psum_scatter(partial, 'z', scatter_dimension=0, tiled=True)  19.7 us
    all_to_all x1, starting transfers between devices, local(): mine = lax.all_to_all(message, EXPERT_AXES, 0, 0, tiled=True)  14.1 us
    pallas_call x1, Pallas kernels, partial_of(): pl.pallas_call(partial_kernel, grid=(width // block,), in_specs=[pl.Block...  6.53 us
    slice x1, matrix products, local(): z = z.reshape(experts, CAP + 1, hidden)[:, :CAP].reshape(slots, hidden)  5.59 us
    all_to_all x1, starting transfers between devices, local(): back = lax.all_to_all(reply, EXPERT_AXES, 0, 0, tiled=True)  5.24 us
    dot_general x1, matrix products, local(): lax.dot_general(dz_in, matrix, (((1,), (1,)), ((), ())), preferred_elemen...  4.98 us
  transfers between devices with their start and end apart: 4, of which 4 were waited for; matrix products, arithmetic and copies ran while one was open for 12% of the time, Pallas kernels for 0%

profile of v4, /device:TPU:1, one launch (start us, length us, event | category | flops | bytes accessed | tf_op | source)
XLA Modules:
  0.0 180.6 jit_solution(17334912769196228434)
XLA Ops:
  7.2 0.0 copy-start.5
  7.2 0.8 copy.24
  8.0 0.8 compare_reduce_fusion
  8.8 0.1 fusion.22
  8.9 1.3 multiply_convert_fusion
  10.3 0.0 copy-done.5
  10.3 0.0 copy-start.7
  10.3 0.0 copy-start.4
  10.3 0.5 fusion.16
  10.8 0.3 reshape.157
  11.0 0.0 copy-done.7
  11.1 0.3 copy-done.4
  11.4 0.6 convolution_convert_fusion
  11.9 0.6 reshape.156
  12.6 0.1 pad.9.clone
  12.7 1.7 maximum_maximum_fusion
  14.3 14.1 %all-to-all-start = ((bf16[32,192,128]{2,1,0:T(8,128)(2,1)}), bf16[32,192,128]{2,1,0:T(8,128)(2,1)S(1)}, u32[]{:S(2)}, u32[]{:S(2)}) async-start(bf16[32,192,128]{2,1,0:T(8,128)(2,1)} %maximum_maximum_fusion), calls=%async_computation | async-start | bytes 3145728 | tf_op jit(solution)/shard_map/all_to_all | solution.py:93
  28.5 0.0 reduce-scatter.2.cloned.1.call-start
  28.6 0.1 fusion.30.spread_ref
  28.7 0.4 fusion.8.order_ref
  29.1 38.6 %all-to-all-done = bf16[32,192,128]{2,1,0:T(8,128)(2,1)S(1)} async-done(((bf16[32,192,128]{2,1,0:T(8,128)(2,1)}), bf16[32,192,128]{2,1,0:T(8,128)(2,1)S(1)}, u32[]{:S(2)}, u32[]{:S(2)}) %all-to-all-start) | async-done | bytes 1572896 | tf_op jit(solution)/shard_map/all_to_all | solution.py:93
  67.7 0.0 copy-start
  67.7 1.0 fusion.49
  68.7 0.3 copy-done
  69.0 0.3 reshape.158.dz_ref
  69.3 2.5 %reshape.161.x_ref = bf16[192,4096]{1,0:T(8,128)(2,1)S(1)} reshape(bf16[32,192,128]{2,1,0:T(8,128)(2,1)} %copy-done) | data formatting | bytes 3145728 | tf_op jit(solution)/shard_map/reshape | solution.py:94
  71.8 6.5 %shard_map.85 = bf16[768,4096]{1,0:T(8,128)(2,1)} custom-call(bf16[192,4096]{1,0:T(8,128)(2,1)S(1)} %reshape.161.x_ref, bf16[160,768]{1,0:T(8,128)(2,1)S(1)} %reshape.158.dz_ref, bf16[768,768]{1,0:T(8,128)(2,1)S(1)} %fusion.8.order_ref, bf16[160,192]{1,0:T(8,128)(2,1)S(1)} %fusion.30.spread_ref), custom_call_target="tpu_custom_call" | custom-call | flops 1434451968 | bytes 9043968 | tf_op jit(solution)/shard_map/pallas_call | solution.py:32
  78.3 0.0 copy-start.2
  78.3 0.0 copy-start.1
  78.3 0.0 reduce-scatter.2.cloned.1.call-update
  78.4 1.0 copy-done.2
  79.4 0.1 reshape.162
  79.5 0.4 copy-done.1
  79.9 2.7 %dot_general.24 = bf16[32,6,4096]{2,1,0:T(8,128)(2,1)} reshape(bf16[32,192,128]{2,1,0:T(8,128)(2,1)S(1)} %copy-done.1) | data formatting | bytes 3145728 | tf_op jit(solution)/shard_map/dot_general | solution.py:110
  82.6 5.6 %fusion.17 = bf16[32,5]{0,1:T(8,128)(2,1)S(1)} fusion(bf16[1,4096,768]{2,1,0:T(8,128)(2,1)} %param.11, bf16[32,6,4096]{2,1,0:T(8,128)(2,1)} %dot_general.24, f32[32,5,768]{2,1,0:T(8,128)S(1)} %reshape.162), kind=kOutput, calls=%fused_computation.18 | convolution fusion | flops 1006878592 | bytes 8356160 | tf_op jit(solution)/shard_map/slice | solution.py:111
  88.2 0.1 copy.29
  88.3 5.0 %fusion.4 = bf16[160,4096]{1,0:T(8,128)(2,1)S(1)} fusion(bf16[160,768]{1,0:T(8,128)(2,1)S(1)} %reshape.158.dz_ref, bf16[1,4096,768]{2,1,0:T(8,128)(2,1)} %param.11), kind=kOutput, calls=%fused_computation.4 | convolution fusion | flops 1007288320 | bytes 7847936 | tf_op jit(solution)/shard_map/dot_general | solution.py:107
  93.3 0.6 reshape.159
  93.9 1.2 fusion.10
  95.1 5.2 %all-to-all-start.1 = ((bf16[32,176,128]{2,1,0:T(8,128)(2,1)}), bf16[32,176,128]{2,1,0:T(8,128)(2,1)S(1)}, u32[]{:S(2)}, u32[]{:S(2)}) async-start(bf16[32,176,128]{2,1,0:T(8,128)(2,1)} %fusion.10), calls=%async_computation.1 | async-start | bytes 2883584 | tf_op jit(solution)/shard_map/all_to_all | solution.py:120
  100.4 36.5 %all-to-all-done.1 = bf16[32,176,128]{2,1,0:T(8,128)(2,1)S(1)} async-done(((bf16[32,176,128]{2,1,0:T(8,128)(2,1)}), bf16[32,176,128]{2,1,0:T(8,128)(2,1)S(1)}, u32[]{:S(2)}, u32[]{:S(2)}) %all-to-all-start.1) | async-done | bytes 1441824 | tf_op jit(solution)/shard_map/all_to_all | solution.py:120
  136.9 1.2 slice.17
  138.0 0.0 copy-start.6
  138.0 2.4 %reshape.160 = bf16[160,4096]{1,0:T(8,128)(2,1)S(1)} reshape(bf16[32,160,128]{2,1,0:T(8,128)(2,1)} %slice.17) | data formatting | bytes 2621440 | tf_op jit(solution)/shard_map/reshape | solution.py:128
  140.5 0.1 reshape.163
  140.6 0.3 fusion.25
  140.9 0.0 copy-done.6
  140.9 0.6 divide_convert_fusion
  141.5 19.7 %reduce-scatter.2.cloned.1.call-done = bf16[64,4096]{1,0:T(8,128)(2,1)} async-done(((bf16[768,4096]{1,0:T(8,128)(2,1)}), bf16[64,4096]{1,0:T(8,128)(2,1)}) %reduce-scatter.2.cloned.1.call-update) | async-done | bytes 524304 | tf_op jit(solution)/shard_map/reduce_scatter | solution.py:104
  161.2 0.0 copy-start.3
  161.2 1.0 constant_dynamic-slice_fusion
  162.3 4.6 %collective-permute-start = (bf16[32,4096]{1,0:T(8,128)(2,1)S(1)}, bf16[32,4096]{1,0:T(8,128)(2,1)S(1)}, u32[]{:S(2)}, u32[]{:S(2)}) collective-permute-start(bf16[32,4096]{1,0:T(8,128)(2,1)S(1)} %constant_dynamic-slice_fusion), channel_id=1, source_target_pairs={{0,384},{384,0},{1,385},{385,1},{2,386},{386,2},{3,387},{387,3},{4... | collective-permute-start | bytes 786440 | tf_op jit(solution)/shard_map/ppermute | solution.py:125
  166.9 1.1 convolution_convert_fusion.1
  168.0 4.9 %collective-permute-done = bf16[32,4096]{1,0:T(8,128)(2,1)S(1)} collective-permute-done((bf16[32,4096]{1,0:T(8,128)(2,1)S(1)}, bf16[32,4096]{1,0:T(8,128)(2,1)S(1)}, u32[]{:S(2)}, u32[]{:S(2)}) %collective-permute-start) | collective-permute-done | bytes 262176 | tf_op jit(solution)/shard_map/ppermute | solution.py:125
  172.9 0.0 copy-done.3
  172.9 0.8 add_bitcast_fusion
  (7 shorter events, 0.1 us)
Async XLA Ops:
  7.2 3.1 %copy-start.5 = (s32[64,8]{0,1:T(8,128)S(1)}, s32[64,8]{0,1:T(8,128)}, u32[]{:S(2)}) copy-start(s32[64,8]{0,1:T(8,128)} %param.8) | copy-start | bytes 6148
  10.3 0.8 copy-start.7
  10.3 1.0 copy-start.4
  14.3 53.3 %all-to-all-start = ((bf16[32,192,128]{2,1,0:T(8,128)(2,1)}), bf16[32,192,128]{2,1,0:T(8,128)(2,1)S(1)}, u32[]{:S(2)}, u32[]{:S(2)}) async-start(bf16[32,192,128]{2,1,0:T(8,128)(2,1)} %maximum_maximum_fusion), calls=%async_computation | async-start | bytes 3145728 | tf_op jit(solution)/shard_map/all_to_all | solution.py:93
  28.5 132.7 %reduce-scatter.2.cloned.1.call-start = ((), (), s32[]{:S(2)}) async-start(), calls=%async_computation.3 | async-start | bytes 6815744 | tf_op jit(solution)/shard_map/reduce_scatter | solution.py:104
  67.7 1.3 copy-start
  78.3 1.0 copy-start.2
  78.3 1.6 copy-start.1
  95.1 41.7 %all-to-all-start.1 = ((bf16[32,176,128]{2,1,0:T(8,128)(2,1)}), bf16[32,176,128]{2,1,0:T(8,128)(2,1)S(1)}, u32[]{:S(2)}, u32[]{:S(2)}) async-start(bf16[32,176,128]{2,1,0:T(8,128)(2,1)} %fusion.10), calls=%async_computation.1 | async-start | bytes 2883584 | tf_op jit(solution)/shard_map/all_to_all | solution.py:120
  138.0 2.8 %copy-start.6 = (bf16[64,8]{0,1:T(8,128)(2,1)S(1)}, bf16[64,8]{0,1:T(8,128)(2,1)}, u32[]{:S(2)}) copy-start(bf16[64,8]{0,1:T(8,128)(2,1)} %param.9) | copy-start | bytes 3076
  161.2 11.7 %copy-start.3 = (bf16[64,4096]{1,0:T(8,128)(2,1)S(1)}, bf16[64,4096]{1,0:T(8,128)(2,1)}, u32[]{:S(2)}) copy-start(bf16[64,4096]{1,0:T(8,128)(2,1)} %reduce-scatter.2.cloned.1.call-done) | copy-start | bytes 1572868
  162.3 10.6 %collective-permute-start = (bf16[32,4096]{1,0:T(8,128)(2,1)S(1)}, bf16[32,4096]{1,0:T(8,128)(2,1)S(1)}, u32[]{:S(2)}, u32[]{:S(2)}) collective-permute-start(bf16[32,4096]{1,0:T(8,128)(2,1)S(1)} %constant_dynamic-slice_fusion), channel_id=1, source_target_pairs={{0,384},{384,0},{1,385},{385,1},{2,386},{386,2},{3,387},{387,3},{4... | collective-permute-start | bytes 786440 | tf_op jit(solution)/shard_map/ppermute | solution.py:125
Sparse Core Ops, SparseCore 0:
  78.5 82.6 reduce-scatter.1

commit v5 on v2

--- a/solution.py
+++ b/solution.py
@@ -31,16 +31,16 @@
     dz = (gate_values.astype(jnp.float32)[..., None] * upstream.astype(jnp.float32)).astype(
         jnp.bfloat16
     )
-    ids = expert_ids.reshape(choices)
-    onehot = (ids[:, None] == jnp.arange(experts, dtype=jnp.int32)[None, :]).astype(jnp.int32)
-    before = jnp.cumsum(onehot, axis=0) - onehot
-    slot = jnp.sum(before * onehot, axis=1)
-    position = jnp.where(ids < experts, ids * CAP + slot, -1)
-    placing = position[:, None] == jnp.arange(slots, dtype=jnp.int32)[None, :]
+    column = jnp.arange(slots, dtype=jnp.int32)
+    named = expert_ids[:, :, None] == (column // CAP)[None, None, :]
+    names = jnp.any(named, axis=1)
+    row = jnp.arange(toks, dtype=jnp.int32)
+    earlier = (row[None, :] < row[:, None]).astype(jnp.bfloat16)
+    rank = jnp.dot(earlier, names.astype(jnp.bfloat16), preferred_element_type=jnp.float32)
+    token_placing = names & (rank == (column % CAP).astype(jnp.float32)[None, :])
+    token_place = token_placing.astype(jnp.bfloat16)
+    placing = (named & token_placing[:, None, :]).reshape(choices, slots)
     place = placing.astype(jnp.bfloat16)
-    token_place = jnp.sum(
-        placing.astype(jnp.int32).reshape(toks, picks, slots), axis=1
-    ).astype(jnp.bfloat16)
 
     send_x = dot_t(token_place, x).astype(jnp.bfloat16)
     send_dz = dot_t(place, dz.reshape(choices, hidden)).astype(jnp.bfloat16)

time: 180 us -> 179 us (level)
  local copies, waits for them, and re-layouts: 13.2 us -> 11.3 us
    unnamed x11 -> x10, local copies, waits for them, and re-layouts: 2.28 us -> 0.31 us
where the time goes in v5:
time: 179 us; the launch traced here: 178 us
  waiting for transfers between devices  106 us (59%)
  starting transfers between devices  24 us (13%)
  matrix products  15.8 us (9%)
  between operations  14.3 us (8%)
  local copies, waits for them, and re-layouts  11.3 us (6%)
  other arithmetic  6.83 us (4%)
    all_to_all x1, waiting for transfers between devices, local(): mine = lax.all_to_all(message, EXPERT_AXES, 0, 0, tiled=True)  39.1 us
    all_to_all x1, waiting for transfers between devices, local(): back = lax.all_to_all(reply, EXPERT_AXES, 0, 0, tiled=True)  36.5 us
    reduce_scatter x1, waiting for transfers between devices, local(): summed = lax.psum_scatter(partial, 'z', scatter_dimension=0, tiled=True)  25.4 us
    all_to_all x1, starting transfers between devices, local(): mine = lax.all_to_all(message, EXPERT_AXES, 0, 0, tiled=True)  14.1 us
    dot_general x3, matrix products, dot_t(): lax.dot_general(a, b, (((0,), (0,)), ((), ())), preferred_element_type=jn...  5.51 us
    all_to_all x1, starting transfers between devices, local(): back = lax.all_to_all(reply, EXPERT_AXES, 0, 0, tiled=True)  5.24 us
    dot_general x1, matrix products, local(): lax.dot_general(dz_in, matrix, (((1,), (1,)), ((), ())), preferred_elemen...  4.98 us
    ppermute x1, waiting for transfers between devices, local(): got = lax.ppermute(give, 'xh', [(0, 1), (1, 0)])  4.89 us
  transfers between devices with their start and end apart: 4, of which 4 were waited for; matrix products, arithmetic and copies ran while one was open for 9% of the time, Pallas kernels for 0%

profile of v5, /device:TPU:1, one launch (start us, length us, event | category | flops | bytes accessed | tf_op | source)
XLA Modules:
  0.0 178.2 jit_solution(7495433430590012941)
XLA Ops:
  7.2 0.0 copy-start.2
  7.2 0.8 copy.18
  8.0 0.8 compare_reduce_fusion
  8.8 0.1 fusion.19
  8.9 1.3 multiply_convert_fusion
  10.3 0.0 copy-done.2
  10.3 0.0 copy-start.4
  10.3 0.0 copy-start.1
  10.3 0.5 fusion.13
  10.8 0.3 reshape.136
  11.0 0.0 copy-done.4
  11.1 0.3 copy-done.1
  11.4 0.6 convolution_convert_fusion.1
  11.9 0.6 reshape.135
  12.6 0.1 pad.9.clone
  12.7 1.7 maximum_maximum_fusion
  14.3 14.1 %all-to-all-start = ((bf16[32,192,128]{2,1,0:T(8,128)(2,1)}), bf16[32,192,128]{2,1,0:T(8,128)(2,1)S(1)}, u32[]{:S(2)}, u32[]{:S(2)}) async-start(bf16[32,192,128]{2,1,0:T(8,128)(2,1)} %maximum_maximum_fusion), calls=%async_computation | async-start | bytes 3145728 | tf_op jit(solution)/shard_map/all_to_all | solution.py:56
  28.5 0.0 reduce-scatter.2.cloned.1.call-start
  28.5 39.1 %all-to-all-done = bf16[32,192,128]{2,1,0:T(8,128)(2,1)S(1)} async-done(((bf16[32,192,128]{2,1,0:T(8,128)(2,1)}), bf16[32,192,128]{2,1,0:T(8,128)(2,1)S(1)}, u32[]{:S(2)}, u32[]{:S(2)}) %all-to-all-start) | async-done | bytes 1572896 | tf_op jit(solution)/shard_map/all_to_all | solution.py:56
  67.7 1.1 slice.17
  68.8 2.4 %reshape.139 = bf16[160,4096]{1,0:T(8,128)(2,1)S(1)} reshape(bf16[32,160,128]{2,1,0:T(8,128)(2,1)} %slice.17) | data formatting | bytes 2621440 | tf_op jit(solution)/shard_map/reshape | solution.py:57
  71.2 0.3 reshape.137
  71.5 4.5 %convolution_convert_fusion = bf16[768,4096]{1,0:T(8,128)(2,1)} fusion(bf16[160,4096]{1,0:T(8,128)(2,1)S(1)} %reshape.139, bf16[160,768]{1,0:T(8,128)(2,1)S(1)} %reshape.137, s32[768]{0:T(1024)S(1)} %fusion.37), kind=kOutput, calls=%fused_computation | convolution fusion | flops 1199235072 | bytes 7851008 | tf_op jit(solution)/shard_map/dot_general | solution.py:13
  75.9 0.0 reduce-scatter.2.cloned.1.call-update
  76.0 4.1 %fusion.16 = bf16[160]{0:T(256)(128)(2,1)S(1)} fusion(bf16[160,4096]{1,0:T(8,128)(2,1)S(1)} %reshape.139, bf16[1,4096,768]{2,1,0:T(8,128)(2,1)} %param.11, bf16[160,768]{1,0:T(8,128)(2,1)S(1)} %reshape.137), kind=kOutput, calls=%fused_computation.20 | convolution fusion | flops 1007001472 | bytes 7848256 | tf_op jit(solution)/shard_map/dot_general | solution.py:72
  80.1 0.1 convert_element_type.108
  80.2 5.0 %fusion.4 = bf16[160,4096]{1,0:T(8,128)(2,1)S(1)} fusion(bf16[160,768]{1,0:T(8,128)(2,1)S(1)} %reshape.137, bf16[1,4096,768]{2,1,0:T(8,128)(2,1)} %param.11), kind=kOutput, calls=%fused_computation.5 | convolution fusion | flops 1007288320 | bytes 7847936 | tf_op jit(solution)/shard_map/dot_general | solution.py:69
  85.2 0.6 reshape.138
  85.8 1.2 fusion.9
  87.0 5.2 %all-to-all-start.1 = ((bf16[32,176,128]{2,1,0:T(8,128)(2,1)}), bf16[32,176,128]{2,1,0:T(8,128)(2,1)S(1)}, u32[]{:S(2)}, u32[]{:S(2)}) async-start(bf16[32,176,128]{2,1,0:T(8,128)(2,1)} %fusion.9), calls=%async_computation.1 | async-start | bytes 2883584 | tf_op jit(solution)/shard_map/all_to_all | solution.py:81
  92.3 36.5 %all-to-all-done.1 = bf16[32,176,128]{2,1,0:T(8,128)(2,1)S(1)} async-done(((bf16[32,176,128]{2,1,0:T(8,128)(2,1)}), bf16[32,176,128]{2,1,0:T(8,128)(2,1)S(1)}, u32[]{:S(2)}, u32[]{:S(2)}) %all-to-all-start.1) | async-done | bytes 1441824 | tf_op jit(solution)/shard_map/all_to_all | solution.py:81
  128.8 1.2 slice.18
  130.0 0.0 copy-start.3
  130.0 2.4 %reshape.140 = bf16[160,4096]{1,0:T(8,128)(2,1)S(1)} reshape(bf16[32,160,128]{2,1,0:T(8,128)(2,1)} %slice.18) | data formatting | bytes 2621440 | tf_op jit(solution)/shard_map/reshape | solution.py:89
  132.4 0.1 reshape.141
  132.5 0.3 fusion.22
  132.8 0.0 copy-done.3
  132.8 0.6 divide_convert_fusion
  133.4 25.4 %reduce-scatter.2.cloned.1.call-done = bf16[64,4096]{1,0:T(8,128)(2,1)} async-done(((bf16[768,4096]{1,0:T(8,128)(2,1)}), bf16[64,4096]{1,0:T(8,128)(2,1)}) %reduce-scatter.2.cloned.1.call-update) | async-done | bytes 524304 | tf_op jit(solution)/shard_map/reduce_scatter | solution.py:66
  158.8 0.0 copy-start
  158.8 1.0 constant_dynamic-slice_fusion
  159.9 4.6 %collective-permute-start = (bf16[32,4096]{1,0:T(8,128)(2,1)S(1)}, bf16[32,4096]{1,0:T(8,128)(2,1)S(1)}, u32[]{:S(2)}, u32[]{:S(2)}) collective-permute-start(bf16[32,4096]{1,0:T(8,128)(2,1)S(1)} %constant_dynamic-slice_fusion), channel_id=1, source_target_pairs={{0,384},{384,0},{1,385},{385,1},{2,386},{386,2},{3,387},{387,3},{4... | collective-permute-start | bytes 786440 | tf_op jit(solution)/shard_map/ppermute | solution.py:86
  164.5 1.1 convolution_convert_fusion.2
  165.6 4.9 %collective-permute-done = bf16[32,4096]{1,0:T(8,128)(2,1)S(1)} collective-permute-done((bf16[32,4096]{1,0:T(8,128)(2,1)S(1)}, bf16[32,4096]{1,0:T(8,128)(2,1)S(1)}, u32[]{:S(2)}, u32[]{:S(2)}) %collective-permute-start) | collective-permute-done | bytes 262176 | tf_op jit(solution)/shard_map/ppermute | solution.py:86
  170.5 0.0 copy-done
  170.5 0.8 add_bitcast_fusion
  (7 shorter events, 0.1 us)
Async XLA Ops:
  7.2 3.1 %copy-start.2 = (s32[64,8]{0,1:T(8,128)S(1)}, s32[64,8]{0,1:T(8,128)}, u32[]{:S(2)}) copy-start(s32[64,8]{0,1:T(8,128)} %param.8) | copy-start | bytes 6148
  10.3 0.8 copy-start.4
  10.3 1.0 copy-start.1
  14.3 53.3 %all-to-all-start = ((bf16[32,192,128]{2,1,0:T(8,128)(2,1)}), bf16[32,192,128]{2,1,0:T(8,128)(2,1)S(1)}, u32[]{:S(2)}, u32[]{:S(2)}) async-start(bf16[32,192,128]{2,1,0:T(8,128)(2,1)} %maximum_maximum_fusion), calls=%async_computation | async-start | bytes 3145728 | tf_op jit(solution)/shard_map/all_to_all | solution.py:56
  28.5 130.3 %reduce-scatter.2.cloned.1.call-start = ((), (), s32[]{:S(2)}) async-start(), calls=%async_computation.3 | async-start | bytes 6815744 | tf_op jit(solution)/shard_map/reduce_scatter | solution.py:66
  87.0 41.7 %all-to-all-start.1 = ((bf16[32,176,128]{2,1,0:T(8,128)(2,1)}), bf16[32,176,128]{2,1,0:T(8,128)(2,1)S(1)}, u32[]{:S(2)}, u32[]{:S(2)}) async-start(bf16[32,176,128]{2,1,0:T(8,128)(2,1)} %fusion.9), calls=%async_computation.1 | async-start | bytes 2883584 | tf_op jit(solution)/shard_map/all_to_all | solution.py:81
  130.0 2.8 %copy-start.3 = (bf16[64,8]{0,1:T(8,128)(2,1)S(1)}, bf16[64,8]{0,1:T(8,128)(2,1)}, u32[]{:S(2)}) copy-start(bf16[64,8]{0,1:T(8,128)(2,1)} %param.9) | copy-start | bytes 3076
  158.8 11.7 %copy-start = (bf16[64,4096]{1,0:T(8,128)(2,1)S(1)}, bf16[64,4096]{1,0:T(8,128)(2,1)}, u32[]{:S(2)}) copy-start(bf16[64,4096]{1,0:T(8,128)(2,1)} %reduce-scatter.2.cloned.1.call-done) | copy-start | bytes 1572868
  159.9 10.6 %collective-permute-start = (bf16[32,4096]{1,0:T(8,128)(2,1)S(1)}, bf16[32,4096]{1,0:T(8,128)(2,1)S(1)}, u32[]{:S(2)}, u32[]{:S(2)}) collective-permute-start(bf16[32,4096]{1,0:T(8,128)(2,1)S(1)} %constant_dynamic-slice_fusion), channel_id=1, source_target_pairs={{0,384},{384,0},{1,385},{385,1},{2,386},{386,2},{3,387},{387,3},{4... | collective-permute-start | bytes 786440 | tf_op jit(solution)/shard_map/ppermute | solution.py:86
Sparse Core Ops, SparseCore 0:
  76.1 82.6 reduce-scatter.1

commit v6 on v5

--- a/solution.py
+++ b/solution.py
@@ -18,7 +18,6 @@
     width = token_rows.shape[1]
     hidden = upstream.shape[2]
     experts = lax.axis_size(EXPERT_AXES)
-    depth = lax.axis_size("z")
     slots = experts * CAP
     choices = toks * picks
     half = hidden // 2
@@ -44,26 +43,43 @@
 
     send_x = dot_t(token_place, x).astype(jnp.bfloat16)
     send_dz = dot_t(place, dz.reshape(choices, hidden)).astype(jnp.bfloat16)
-    pad = (-(x_lines + dz_lines)) % 16
-    message = jnp.concatenate(
+    cut = width // 2
+    cut_lines = x_lines // 2
+    pad = (-(cut_lines + dz_lines)) % 16
+    first = jnp.concatenate(
         [
-            send_x.reshape(experts, x_lines, LANE),
+            send_x[:, :cut].reshape(experts, cut_lines, LANE),
             send_dz.reshape(experts, dz_lines, LANE),
             jnp.zeros((experts, pad, LANE), jnp.bfloat16),
         ],
         axis=1,
     )
-    mine = lax.all_to_all(message, EXPERT_AXES, 0, 0, tiled=True)
-    x_in = mine[:, :x_lines].reshape(slots, width)
-    dz_in = mine[:, x_lines : x_lines + dz_lines].reshape(slots, hidden)
+    second = send_x[:, cut:].reshape(experts, cut_lines, LANE)
+    swap = [(0, 1), (1, 0)]
+    mine = lax.all_to_all(first, EXPERT_AXES, 0, 0, tiled=True)
+    mine, second = lax.optimization_barrier((mine, second))
+    other = lax.ppermute(mine, "xh", swap)
+    mine_late = lax.all_to_all(second, EXPERT_AXES, 0, 0, tiled=True)
+    other_late = lax.ppermute(mine_late, "xh", swap)
 
-    unit = jnp.arange(hidden)
-    shard = hidden // (2 * depth)
-    source = (unit // shard % 2) * half + unit // (2 * shard) * shard + unit % shard
-    reorder = (unit[:, None] == source[None, :]).astype(jnp.bfloat16)
-    dz_ordered = jnp.dot(dz_in, reorder, preferred_element_type=jnp.float32).astype(jnp.bfloat16)
-    partial = dot_t(dz_ordered, x_in).astype(jnp.bfloat16)
-    summed = lax.psum_scatter(partial, "z", scatter_dimension=0, tiled=True)
+    def unpack(early, late):
+        rows = jnp.concatenate(
+            [early[:, :cut_lines].reshape(slots, cut), late.reshape(slots, cut)], axis=1
+        )
+        return rows, early[:, cut_lines : cut_lines + dz_lines].reshape(slots, hidden)
+
+    x_in, dz_in = unpack(mine, mine_late)
+    x_other, dz_other = unpack(other, other_late)
+    at = lax.axis_index("xh") * half
+    dz_both = jnp.concatenate(
+        [
+            lax.dynamic_slice_in_dim(dz_in, at, half, 1),
+            lax.dynamic_slice_in_dim(dz_other, at, half, 1),
+        ],
+        axis=0,
+    )
+    partial = dot_t(dz_both, jnp.concatenate([x_in, x_other], axis=0)).astype(jnp.bfloat16)
+    weight_grads = lax.psum_scatter(partial, "z", scatter_dimension=0, tiled=True)
 
     matrix = weight[0]
     row_grads = lax.dot_general(
@@ -80,12 +96,6 @@
     )
     back = lax.all_to_all(reply, EXPERT_AXES, 0, 0, tiled=True)
 
-    side = lax.axis_index("xh")
-    keep = lax.dynamic_slice_in_dim(summed, side * shard, shard, 0)
-    give = lax.dynamic_slice_in_dim(summed, (1 - side) * shard, shard, 0)
-    got = lax.ppermute(give, "xh", [(0, 1), (1, 0)])
-    weight_grads = keep.astype(jnp.float32) + got.astype(jnp.float32)
-
     back_rows = back[:, :x_lines].reshape(slots, width)
     back_terms = back[:, x_lines, :CAP].reshape(slots).astype(jnp.float32)
     token_grads = jnp.dot(token_place, back_rows, preferred_element_type=jnp.float32).astype(
@@ -95,7 +105,7 @@
     gate_grads = (picked.reshape(toks, picks) / gate_values.astype(jnp.float32)).astype(
         jnp.bfloat16
     )
-    return token_grads, gate_grads, weight_grads.T[None]
+    return token_grads, gate_grads, weight_grads.astype(jnp.float32).T[None]
 
 
 def solution(mesh):

time: 179 us -> 183 us (1.022)
  the two profiles are of different devices: /device:TPU:1 before, /device:TPU:10 now
where the time goes in v6:
time: 183 us; the launch traced here: 182 us
  waiting for transfers between devices  65.4 us (36%)
  blocking collectives  44.6 us (24%)
  starting transfers between devices  21.9 us (12%)
  matrix products  16.6 us (9%)
  between operations  14.3 us (8%)
  local copies, waits for them, and re-layouts  13.1 us (7%)
  other arithmetic  6.16 us (3%)
    all_to_all x1, blocking collectives, local(): back = lax.all_to_all(reply, EXPERT_AXES, 0, 0, tiled=True)  44.6 us
    all_to_all x1, waiting for transfers between devices, local(): mine = lax.all_to_all(first, EXPERT_AXES, 0, 0, tiled=True)  24.2 us
    all_to_all x1, waiting for transfers between devices, local(): mine_late = lax.all_to_all(second, EXPERT_AXES, 0, 0, tiled=True)  17.1 us
    all_to_all x1, starting transfers between devices, local(): mine = lax.all_to_all(first, EXPERT_AXES, 0, 0, tiled=True)  13 us
    ppermute x1, waiting for transfers between devices, local(): other_late = lax.ppermute(mine_late, 'xh', swap)  9.46 us
    reduce_scatter x1, waiting for transfers between devices, local(): lax.psum_scatter(partial, 'z', scatter_dimension=0, tiled=True)  7.52 us
    ppermute x1, waiting for transfers between devices, local(): other = lax.ppermute(mine, 'xh', swap)  7.14 us
    dot_general x3, matrix products, dot_t(): lax.dot_general(a, b, (((0,), (0,)), ((), ())), preferred_element_type=jn...  5.84 us
  transfers between devices with their start and end apart: 5, of which 5 were waited for; matrix products, arithmetic and copies ran while one was open for 12% of the time, Pallas kernels for 0%

profile of v6, /device:TPU:10, one launch (start us, length us, event | category | flops | bytes accessed | tf_op | source)
XLA Modules:
  0.0 182.0 jit_solution(12199034191229263322)
XLA Ops:
  7.2 0.0 copy-start.1
  7.2 0.8 copy.18
  8.0 0.8 compare_reduce_fusion
  8.8 0.1 fusion.21
  8.9 1.3 multiply_convert_fusion
  10.3 0.0 copy-done.1
  10.3 0.0 copy-start.3
  10.3 0.0 copy-start
  10.3 0.5 fusion.17
  10.8 0.3 reshape.108
  11.0 0.0 copy-done.3
  11.1 0.3 copy-done
  11.4 0.6 convolution_convert_fusion.1
  11.9 0.1 fusion.37
  12.0 0.3 reshape.107
  12.3 0.1 pad.14.clone
  12.4 1.2 maximum_maximum_fusion
  13.6 13.0 %all-to-all-start = ((bf16[32,112,128]{2,1,0:T(8,128)(2,1)}), bf16[32,112,128]{2,1,0:T(8,128)(2,1)S(1)}, u32[]{:S(2)}, u32[]{:S(2)}) async-start(bf16[32,112,128]{2,1,0:T(8,128)(2,1)} %maximum_maximum_fusion), calls=%async_computation | async-start | bytes 1835008 | tf_op jit(solution)/shard_map/all_to_all | solution.py:59
  26.7 1.2 reshape.109
  27.8 24.2 %all-to-all-done = bf16[32,112,128]{2,1,0:T(8,128)(2,1)S(1)} async-done(((bf16[32,112,128]{2,1,0:T(8,128)(2,1)}), bf16[32,112,128]{2,1,0:T(8,128)(2,1)S(1)}, u32[]{:S(2)}, u32[]{:S(2)}) %all-to-all-start) | async-done | bytes 917536 | tf_op jit(solution)/shard_map/all_to_all | solution.py:59
  52.0 5.0 %all-to-all-start.1 = ((bf16[32,80,128]{2,1,0:T(8,128)(2,1)}), bf16[32,80,128]{2,1,0:T(8,128)(2,1)S(1)}, u32[]{:S(2)}, u32[]{:S(2)}) async-start(bf16[32,80,128]{2,1,0:T(8,128)(2,1)} %reshape.109), calls=%async_computation.1 | async-start | bytes 1310720 | tf_op jit(solution)/shard_map/all_to_all | solution.py:62
  57.0 0.0 reduce-scatter.2.cloned.1.call-start
  57.0 1.9 %collective-permute-start = (bf16[32,112,128]{2,1,0:T(8,128)(2,1)S(1)}, bf16[32,112,128]{2,1,0:T(8,128)(2,1)}, u32[]{:S(2)}, u32[]{:S(2)}) collective-permute-start(bf16[32,112,128]{2,1,0:T(8,128)(2,1)S(1)} %all-to-all-done), channel_id=1, source_target_pairs={{0,384},{384,0},{1,385},{385,1},{2,386},{386,2},{3,387},{387,3},{4... | collective-permute-start | bytes 2752520 | tf_op jit(solution)/shard_map/ppermute | solution.py:61
  59.0 0.3 reshape.112
  59.3 0.3 reshape.110
  59.6 17.1 %all-to-all-done.1 = bf16[32,80,128]{2,1,0:T(8,128)(2,1)S(1)} async-done(((bf16[32,80,128]{2,1,0:T(8,128)(2,1)}), bf16[32,80,128]{2,1,0:T(8,128)(2,1)S(1)}, u32[]{:S(2)}, u32[]{:S(2)}) %all-to-all-start.1) | async-done | bytes 655392 | tf_op jit(solution)/shard_map/all_to_all | solution.py:62
  76.7 1.9 %collective-permute-start.1 = (bf16[32,80,128]{2,1,0:T(8,128)(2,1)S(1)}, bf16[32,80,128]{2,1,0:T(8,128)(2,1)S(1)}, u32[]{:S(2)}, u32[]{:S(2)}) collective-permute-start(bf16[32,80,128]{2,1,0:T(8,128)(2,1)S(1)} %all-to-all-done.1), channel_id=1, source_target_pairs={{0,384},{384,0},{1,385},{385,1},{2,386},{386,2},{3,387},{387,3},{4... | collective-permute-start | bytes 1966088 | tf_op jit(solution)/shard_map/ppermute | solution.py:63
  78.6 0.9 constant_dynamic-update-slice_fusion.1
  79.6 7.1 %collective-permute-done = bf16[32,112,128]{2,1,0:T(8,128)(2,1)} collective-permute-done((bf16[32,112,128]{2,1,0:T(8,128)(2,1)S(1)}, bf16[32,112,128]{2,1,0:T(8,128)(2,1)}, u32[]{:S(2)}, u32[]{:S(2)}) %collective-permute-start) | collective-permute-done | bytes 917536 | tf_op jit(solution)/shard_map/ppermute | solution.py:61
  86.7 1.0 slice.36
  87.7 0.3 reshape.115
  87.9 1.1 slice.37
  89.1 0.3 reshape.116
  89.4 0.3 reshape.113
  89.7 0.9 constant_dynamic-update-slice_fusion
  90.6 9.5 %collective-permute-done.1 = bf16[32,80,128]{2,1,0:T(8,128)(2,1)S(1)} collective-permute-done((bf16[32,80,128]{2,1,0:T(8,128)(2,1)S(1)}, bf16[32,80,128]{2,1,0:T(8,128)(2,1)S(1)}, u32[]{:S(2)}, u32[]{:S(2)}) %collective-permute-start.1) | collective-permute-done | bytes 655392 | tf_op jit(solution)/shard_map/ppermute | solution.py:63
  100.0 0.3 reshape.117
  100.3 4.8 %convolution_convert_fusion = bf16[384,4096]{1,0:T(8,128)(2,1)} fusion(bf16[160,2048]{1,0:T(8,128)(2,1)S(1)} %reshape.117, bf16[160,2048]{1,0:T(8,128)(2,1)S(1)} %reshape.116, bf16[160,4096]{1,0:T(8,128)(2,1)} %constant_dynamic-update-slice_fusion, bf16[160,384]{1,0:T(8,128)(2,1)S(1)} %constant_dynamic-slice_fusion, ...), kind=kOutput, calls=%fused_computation.4 | convolution fusion | flops 1016561664 | bytes 6012928 | tf_op jit(solution)/shard_map/dot_general | solution.py:13
  105.2 0.0 reduce-scatter.2.cloned.1.call-update
  105.2 5.0 %fusion.4 = bf16[160,4096]{1,0:T(8,128)(2,1)S(1)} fusion(bf16[160,768]{1,0:T(8,128)(2,1)S(1)} %reshape.110, bf16[1,4096,768]{2,1,0:T(8,128)(2,1)} %param.11), kind=kOutput, calls=%fused_computation.5 | convolution fusion | flops 1007288320 | bytes 7847936 | tf_op jit(solution)/shard_map/dot_general | solution.py:85
  110.2 0.6 reshape.111
  110.8 4.5 %fusion.18 = bf16[160]{0:T(256)(128)(2,1)S(1)} fusion(bf16[160,4096]{1,0:T(8,128)(2,1)} %constant_dynamic-update-slice_fusion, bf16[1,4096,768]{2,1,0:T(8,128)(2,1)} %param.11, bf16[160,768]{1,0:T(8,128)(2,1)S(1)} %reshape.110), kind=kOutput, calls=%fused_computation.20 | convolution fusion | flops 1007001472 | bytes 7848256 | tf_op jit(solution)/shard_map/dot_general | solution.py:88
  115.3 0.1 convert_element_type.96
  115.4 0.1 fusion.13
  115.5 44.6 %all_to_all.15 = bf16[32,176,128]{2,1,0:T(8,128)(2,1)S(1)} all-to-all(bf16[32,176,128]{2,1,0:T(8,128)(2,1)S(1)} %fusion.13), channel_id=1, replica_groups=mesh['xh'=2,'z'=12,'y'=8,'xl'=2,'c'=2] {'y','xl','c'}, dimensions={0} | all-to-all | bytes 2883584 | tf_op jit(solution)/shard_map/all_to_all | solution.py:97
  160.1 1.2 slice.34
  161.3 0.0 copy-start.2
  161.3 2.4 %reshape.114 = bf16[160,4096]{1,0:T(8,128)(2,1)S(1)} reshape(bf16[32,160,128]{2,1,0:T(8,128)(2,1)} %slice.34) | data formatting | bytes 2621440 | tf_op jit(solution)/shard_map/reshape | solution.py:99
  163.7 0.1 reshape.118
  163.8 0.3 fusion.24
  164.1 0.0 copy-done.2
  164.1 0.6 divide_convert_fusion
  164.7 1.1 convolution_convert_fusion.2
  165.8 7.5 %reduce-scatter.2.cloned.1.call-done = bf16[32,4096]{1,0:T(8,128)(2,1)} async-done(((bf16[384,4096]{1,0:T(8,128)(2,1)}), bf16[32,4096]{1,0:T(8,128)(2,1)}) %reduce-scatter.2.cloned.1.call-update) | async-done | bytes 262160 | tf_op jit(solution)/shard_map/reduce_scatter | solution.py:82
  173.3 1.8 convert_bitcast_fusion
  (9 shorter events, 0.2 us)
Async XLA Ops:
  7.2 3.1 %copy-start.1 = (s32[64,8]{0,1:T(8,128)S(1)}, s32[64,8]{0,1:T(8,128)}, u32[]{:S(2)}) copy-start(s32[64,8]{0,1:T(8,128)} %param.8) | copy-start | bytes 6148
  10.3 0.8 copy-start.3
  10.3 1.0 copy-start
  13.6 38.4 %all-to-all-start = ((bf16[32,112,128]{2,1,0:T(8,128)(2,1)}), bf16[32,112,128]{2,1,0:T(8,128)(2,1)S(1)}, u32[]{:S(2)}, u32[]{:S(2)}) async-start(bf16[32,112,128]{2,1,0:T(8,128)(2,1)} %maximum_maximum_fusion), calls=%async_computation | async-start | bytes 1835008 | tf_op jit(solution)/shard_map/all_to_all | solution.py:59
  52.0 24.7 %all-to-all-start.1 = ((bf16[32,80,128]{2,1,0:T(8,128)(2,1)}), bf16[32,80,128]{2,1,0:T(8,128)(2,1)S(1)}, u32[]{:S(2)}, u32[]{:S(2)}) async-start(bf16[32,80,128]{2,1,0:T(8,128)(2,1)} %reshape.109), calls=%async_computation.1 | async-start | bytes 1310720 | tf_op jit(solution)/shard_map/all_to_all | solution.py:62
  57.0 116.4 %reduce-scatter.2.cloned.1.call-start = ((), (), s32[]{:S(2)}) async-start(), calls=%async_computation.4 | async-start | bytes 3407872 | tf_op jit(solution)/shard_map/reduce_scatter | solution.py:82
  57.0 29.7 %collective-permute-start = (bf16[32,112,128]{2,1,0:T(8,128)(2,1)S(1)}, bf16[32,112,128]{2,1,0:T(8,128)(2,1)}, u32[]{:S(2)}, u32[]{:S(2)}) collective-permute-start(bf16[32,112,128]{2,1,0:T(8,128)(2,1)S(1)} %all-to-all-done), channel_id=1, source_target_pairs={{0,384},{384,0},{1,385},{385,1},{2,386},{386,2},{3,387},{387,3},{4... | collective-permute-start | bytes 2752520 | tf_op jit(solution)/shard_map/ppermute | solution.py:61
  76.7 23.3 %collective-permute-start.1 = (bf16[32,80,128]{2,1,0:T(8,128)(2,1)S(1)}, bf16[32,80,128]{2,1,0:T(8,128)(2,1)S(1)}, u32[]{:S(2)}, u32[]{:S(2)}) collective-permute-start(bf16[32,80,128]{2,1,0:T(8,128)(2,1)S(1)} %all-to-all-done.1), channel_id=1, source_target_pairs={{0,384},{384,0},{1,385},{385,1},{2,386},{386,2},{3,387},{387,3},{4... | collective-permute-start | bytes 1966088 | tf_op jit(solution)/shard_map/ppermute | solution.py:63
  161.3 2.8 %copy-start.2 = (bf16[64,8]{0,1:T(8,128)(2,1)S(1)}, bf16[64,8]{0,1:T(8,128)(2,1)}, u32[]{:S(2)}) copy-start(bf16[64,8]{0,1:T(8,128)(2,1)} %param.9) | copy-start | bytes 3076
Sparse Core Ops, SparseCore 0:
  105.3 67.9 reduce-scatter.1

commit v7 on v5

--- a/solution.py
+++ b/solution.py
@@ -25,12 +25,6 @@
     x_lines = CAP * width // LANE
     dz_lines = CAP * hidden // LANE
 
-    x = (row_scales.astype(jnp.float32)[:, None] * token_rows.astype(jnp.float32)).astype(
-        jnp.bfloat16
-    )
-    dz = (gate_values.astype(jnp.float32)[..., None] * upstream.astype(jnp.float32)).astype(
-        jnp.bfloat16
-    )
     column = jnp.arange(slots, dtype=jnp.int32)
     named = expert_ids[:, :, None] == (column // CAP)[None, None, :]
     names = jnp.any(named, axis=1)
@@ -40,10 +34,11 @@
     token_placing = names & (rank == (column % CAP).astype(jnp.float32)[None, :])
     token_place = token_placing.astype(jnp.bfloat16)
     placing = (named & token_placing[:, None, :]).reshape(choices, slots)
-    place = placing.astype(jnp.bfloat16)
 
-    send_x = dot_t(token_place, x).astype(jnp.bfloat16)
-    send_dz = dot_t(place, dz.reshape(choices, hidden)).astype(jnp.bfloat16)
+    scaled_place = jnp.where(token_placing, row_scales[:, None], 0)
+    gated_place = jnp.where(placing, gate_values.reshape(choices, 1), 0)
+    send_x = dot_t(scaled_place, token_rows).astype(jnp.bfloat16)
+    send_dz = dot_t(gated_place, upstream.reshape(choices, hidden)).astype(jnp.bfloat16)
     pad = (-(x_lines + dz_lines)) % 16
     message = jnp.concatenate(
         [

time: 179 us -> 181 us (1.011)
  waiting for transfers between devices: 106 us -> 102 us
  local copies, waits for them, and re-layouts: 11.3 us -> 13.9 us
  matrix products: 15.8 us -> 18.2 us
    reduce_scatter x1, waiting for transfers between devices: 25.4 us -> 21.3 us  [local(): summed = lax.psum_scatter(partial, 'z', scatter_dimension=0, tiled=True)]
    dot_general x3, matrix products: 5.51 us -> 7.78 us  [dot_t(): lax.dot_general(a, b, (((0,), (0,)), ((), ())), preferred_element_type=jn...]
  transfers between devices with their start and end apart: 4 -> 4, of which waited for: 4 -> 4; matrix products, arithmetic and copies ran while one was open for 9% -> 11% of each run, Pallas kernels for 0% -> 0%
where the time goes in v7:
time: 181 us
  waiting for transfers between devices  102 us (56%)
  starting transfers between devices  24 us (13%)
  matrix products  18.2 us (10%)
  between operations  14.2 us (8%)
  local copies, waits for them, and re-layouts  13.9 us (8%)
  other arithmetic  8.52 us (5%)
    all_to_all x1, waiting for transfers between devices, local(): mine = lax.all_to_all(message, EXPERT_AXES, 0, 0, tiled=True)  39.1 us
    all_to_all x1, waiting for transfers between devices, local(): back = lax.all_to_all(reply, EXPERT_AXES, 0, 0, tiled=True)  36.5 us
    reduce_scatter x1, waiting for transfers between devices, local(): summed = lax.psum_scatter(partial, 'z', scatter_dimension=0, tiled=True)  21.3 us
    all_to_all x1, starting transfers between devices, local(): mine = lax.all_to_all(message, EXPERT_AXES, 0, 0, tiled=True)  14.1 us
    dot_general x3, matrix products, dot_t(): lax.dot_general(a, b, (((0,), (0,)), ((), ())), preferred_element_type=jn...  7.78 us
    all_to_all x1, starting transfers between devices, local(): back = lax.all_to_all(reply, EXPERT_AXES, 0, 0, tiled=True)  5.24 us
    dot_general x1, matrix products, local(): lax.dot_general(dz_in, matrix, (((1,), (1,)), ((), ())), preferred_elemen...  5.13 us
    ppermute x1, waiting for transfers between devices, local(): got = lax.ppermute(give, 'xh', [(0, 1), (1, 0)])  4.88 us
  transfers between devices with their start and end apart: 4, of which 4 were waited for; matrix products, arithmetic and copies ran while one was open for 11% of the time, Pallas kernels for 0%

profile of v7, /device:TPU:1, one launch (start us, length us, event | category | flops | bytes accessed | tf_op | source)
XLA Modules:
  0.0 180.7 jit_solution(10839586392708826107)
XLA Ops:
  7.2 0.0 copy-start
  7.2 0.0 copy-start.4
  7.2 0.0 copy-start.6
  7.2 0.0 copy-start.5
  7.2 0.9 compare_reduce_fusion
  8.2 0.1 fusion.19
  8.3 0.0 copy-done
  8.3 1.3 fusion.13
  9.6 1.0 reshape.153
  10.6 0.0 copy-done.5
  10.6 0.0 copy-done.4
  10.6 0.0 copy-done.6
  10.6 0.6 convolution_convert_fusion.1
  11.2 0.6 reshape.152
  11.9 0.1 pad.9.clone
  12.0 2.6 %maximum_maximum_fusion = bf16[32,192,128]{2,1,0:T(8,128)(2,1)} fusion(bf16[32,30,128]{2,1,0:T(8,128)(2,1)} %reshape.153, bf16[32,160,128]{2,1,0:T(8,128)(2,1)S(1)} %reshape.152, bf16[192]{0:T(256)(128)(2,1)S(1)} %pad.9.clone), kind=kLoop, calls=%fused_computation.12 | loop fusion | flops 4718592 | bytes 3129728 | tf_op jit(solution)/shard_map/concatenate | solution.py:43
  14.6 14.1 %all-to-all-start = ((bf16[32,192,128]{2,1,0:T(8,128)(2,1)}), bf16[32,192,128]{2,1,0:T(8,128)(2,1)S(1)}, u32[]{:S(2)}, u32[]{:S(2)}) async-start(bf16[32,192,128]{2,1,0:T(8,128)(2,1)} %maximum_maximum_fusion), calls=%async_computation | async-start | bytes 3145728 | tf_op jit(solution)/shard_map/all_to_all | solution.py:51
  28.7 0.0 reduce-scatter.2.cloned.1.call-start
  28.8 39.1 %all-to-all-done = bf16[32,192,128]{2,1,0:T(8,128)(2,1)S(1)} async-done(((bf16[32,192,128]{2,1,0:T(8,128)(2,1)}), bf16[32,192,128]{2,1,0:T(8,128)(2,1)S(1)}, u32[]{:S(2)}, u32[]{:S(2)}) %all-to-all-start) | async-done | bytes 1572896 | tf_op jit(solution)/shard_map/all_to_all | solution.py:51
  67.9 1.2 slice.17
  69.0 3.2 %reshape.156 = bf16[160,4096]{1,0:T(8,128)(2,1)} reshape(bf16[32,160,128]{2,1,0:T(8,128)(2,1)} %slice.17) | data formatting | bytes 2621440 | tf_op jit(solution)/shard_map/reshape | solution.py:52
  72.3 0.3 reshape.154
  72.6 0.0 copy-start.2
  72.6 5.9 %convolution_convert_fusion = bf16[768,4096]{1,0:T(8,128)(2,1)} fusion(bf16[160,4096]{1,0:T(8,128)(2,1)} %reshape.156, bf16[160,768]{1,0:T(8,128)(2,1)S(1)} %reshape.154, s32[768]{0:T(1024)S(1)} %fusion.43), kind=kOutput, calls=%fused_computation | convolution fusion | flops 1199235072 | bytes 7851008 | tf_op jit(solution)/shard_map/dot_general | solution.py:13
  78.5 0.0 copy-start.1
  78.5 0.0 reduce-scatter.2.cloned.1.call-update
  78.5 0.0 copy-done.2
  78.5 1.3 copy-done.1
  79.8 4.1 %fusion.16 = bf16[160]{0:T(256)(128)(2,1)S(1)} fusion(bf16[160,4096]{1,0:T(8,128)(2,1)S(1)} %copy-done.1, bf16[1,4096,768]{2,1,0:T(8,128)(2,1)} %param.11, bf16[160,768]{1,0:T(8,128)(2,1)S(1)} %reshape.154), kind=kOutput, calls=%fused_computation.19 | convolution fusion | flops 1007001472 | bytes 7848256 | tf_op jit(solution)/shard_map/dot_general | solution.py:67
  83.8 0.1 convert_element_type.90
  84.0 5.1 %fusion.4 = bf16[160,4096]{1,0:T(8,128)(2,1)S(1)} fusion(bf16[160,768]{1,0:T(8,128)(2,1)} %copy-done.2, bf16[1,4096,768]{2,1,0:T(8,128)(2,1)} %param.11), kind=kOutput, calls=%fused_computation.5 | convolution fusion | flops 1007288320 | bytes 7847936 | tf_op jit(solution)/shard_map/dot_general | solution.py:64
  89.1 0.6 reshape.155
  89.8 1.2 fusion.9
  91.0 5.2 %all-to-all-start.1 = ((bf16[32,176,128]{2,1,0:T(8,128)(2,1)}), bf16[32,176,128]{2,1,0:T(8,128)(2,1)S(1)}, u32[]{:S(2)}, u32[]{:S(2)}) async-start(bf16[32,176,128]{2,1,0:T(8,128)(2,1)} %fusion.9), calls=%async_computation.1 | async-start | bytes 2883584 | tf_op jit(solution)/shard_map/all_to_all | solution.py:76
  96.2 36.5 %all-to-all-done.1 = bf16[32,176,128]{2,1,0:T(8,128)(2,1)S(1)} async-done(((bf16[32,176,128]{2,1,0:T(8,128)(2,1)}), bf16[32,176,128]{2,1,0:T(8,128)(2,1)S(1)}, u32[]{:S(2)}, u32[]{:S(2)}) %all-to-all-start.1) | async-done | bytes 1441824 | tf_op jit(solution)/shard_map/all_to_all | solution.py:76
  132.7 1.2 slice.18
  133.9 2.4 %reshape.157 = bf16[160,4096]{1,0:T(8,128)(2,1)S(1)} reshape(bf16[32,160,128]{2,1,0:T(8,128)(2,1)} %slice.18) | data formatting | bytes 2621440 | tf_op jit(solution)/shard_map/reshape | solution.py:84
  136.3 0.7 fusion.31
  136.9 0.8 reshape.158
  137.7 1.0 fusion.23
  138.7 1.3 divide_convert_fusion
  140.0 21.3 %reduce-scatter.2.cloned.1.call-done = bf16[64,4096]{1,0:T(8,128)(2,1)} async-done(((bf16[768,4096]{1,0:T(8,128)(2,1)}), bf16[64,4096]{1,0:T(8,128)(2,1)}) %reduce-scatter.2.cloned.1.call-update) | async-done | bytes 524304 | tf_op jit(solution)/shard_map/reduce_scatter | solution.py:61
  161.3 0.0 copy-start.3
  161.3 1.0 constant_dynamic-slice_fusion
  162.4 4.6 %collective-permute-start = (bf16[32,4096]{1,0:T(8,128)(2,1)S(1)}, bf16[32,4096]{1,0:T(8,128)(2,1)S(1)}, u32[]{:S(2)}, u32[]{:S(2)}) collective-permute-start(bf16[32,4096]{1,0:T(8,128)(2,1)S(1)} %constant_dynamic-slice_fusion), channel_id=1, source_target_pairs={{0,384},{384,0},{1,385},{385,1},{2,386},{386,2},{3,387},{387,3},{4... | collective-permute-start | bytes 786440 | tf_op jit(solution)/shard_map/ppermute | solution.py:81
  167.0 1.1 convolution_convert_fusion.2
  168.1 4.9 %collective-permute-done = bf16[32,4096]{1,0:T(8,128)(2,1)S(1)} collective-permute-done((bf16[32,4096]{1,0:T(8,128)(2,1)S(1)}, bf16[32,4096]{1,0:T(8,128)(2,1)S(1)}, u32[]{:S(2)}, u32[]{:S(2)}) %collective-permute-start) | collective-permute-done | bytes 262176 | tf_op jit(solution)/shard_map/ppermute | solution.py:81
  173.0 0.0 copy-done.3
  173.0 0.8 add_bitcast_fusion
  (5 shorter events, 0.0 us)
Async XLA Ops:
  7.2 1.2 copy-start
  7.2 3.4 %copy-start.4 = (bf16[64,4096]{1,0:T(8,128)(2,1)S(1)}, bf16[64,4096]{1,0:T(8,128)(2,1)}, u32[]{:S(2)}) copy-start(bf16[64,4096]{1,0:T(8,128)(2,1)} %param.6) | copy-start | bytes 1572868
  7.2 3.4 %copy-start.6 = (bf16[64]{0:T(256)(128)(2,1)S(1)}, bf16[64]{0:T(256)(128)(2,1)}, u32[]{:S(2)}) copy-start(bf16[64]{0:T(256)(128)(2,1)} %param.7) | copy-start | bytes 388
  7.2 3.4 %copy-start.5 = (s32[160]{0:T(256)}, s32[160]{0:T(256)S(1)}, u32[]{:S(2)}) copy-start(s32[160]{0:T(256)S(1)} %and_select_fusion.1) | copy-start | bytes 1924
  14.6 53.3 %all-to-all-start = ((bf16[32,192,128]{2,1,0:T(8,128)(2,1)}), bf16[32,192,128]{2,1,0:T(8,128)(2,1)S(1)}, u32[]{:S(2)}, u32[]{:S(2)}) async-start(bf16[32,192,128]{2,1,0:T(8,128)(2,1)} %maximum_maximum_fusion), calls=%async_computation | async-start | bytes 3145728 | tf_op jit(solution)/shard_map/all_to_all | solution.py:51
  28.7 132.6 %reduce-scatter.2.cloned.1.call-start = ((), (), s32[]{:S(2)}) async-start(), calls=%async_computation.3 | async-start | bytes 6815744 | tf_op jit(solution)/shard_map/reduce_scatter | solution.py:61
  72.6 5.9 %copy-start.2 = (bf16[160,768]{1,0:T(8,128)(2,1)}, bf16[160,768]{1,0:T(8,128)(2,1)S(1)}, u32[]{:S(2)}) copy-start(bf16[160,768]{1,0:T(8,128)(2,1)S(1)} %reshape.154) | copy-start | bytes 737284
  78.5 1.3 copy-start.1
  91.0 41.7 %all-to-all-start.1 = ((bf16[32,176,128]{2,1,0:T(8,128)(2,1)}), bf16[32,176,128]{2,1,0:T(8,128)(2,1)S(1)}, u32[]{:S(2)}, u32[]{:S(2)}) async-start(bf16[32,176,128]{2,1,0:T(8,128)(2,1)} %fusion.9), calls=%async_computation.1 | async-start | bytes 2883584 | tf_op jit(solution)/shard_map/all_to_all | solution.py:76
  161.3 11.7 %copy-start.3 = (bf16[64,4096]{1,0:T(8,128)(2,1)S(1)}, bf16[64,4096]{1,0:T(8,128)(2,1)}, u32[]{:S(2)}) copy-start(bf16[64,4096]{1,0:T(8,128)(2,1)} %reduce-scatter.2.cloned.1.call-done) | copy-start | bytes 1572868
  162.4 10.6 %collective-permute-start = (bf16[32,4096]{1,0:T(8,128)(2,1)S(1)}, bf16[32,4096]{1,0:T(8,128)(2,1)S(1)}, u32[]{:S(2)}, u32[]{:S(2)}) collective-permute-start(bf16[32,4096]{1,0:T(8,128)(2,1)S(1)} %constant_dynamic-slice_fusion), channel_id=1, source_target_pairs={{0,384},{384,0},{1,385},{385,1},{2,386},{386,2},{3,387},{387,3},{4... | collective-permute-start | bytes 786440 | tf_op jit(solution)/shard_map/ppermute | solution.py:81
Sparse Core Ops, SparseCore 0:
  78.6 82.6 reduce-scatter.1
